TPU v7x, 32 devices: a whole 2x2x4 slice. The times are simulated.
32 devices in a mesh: pb: 8 (over y, x, core), pa: 4 (over z).
Axes of the slice: x: 2, y: 2, z: 4, core: 2. Of those that a mesh axis runs over, the one named last changes fastest.
Arguments:
- hidden: bfloat16 [32, 128, 768], P(('pb', 'pa')), may hold values from -6 to 6
- encoder: bfloat16 [32, 4, 384, 768], P('pb', 'pa'), may hold values from -6 to 6
- lengths: int32 [32, 4], P('pb', 'pa'), may hold values from 1 to 384, 1152 in all within a row
- w_sq: bfloat16 [768, 768], replicated, may hold values from -0.21875 to 0.21875
- w_sk: bfloat16 [768, 768], replicated, may hold values from -0.21875 to 0.21875
- w_sv: bfloat16 [768, 768], replicated, may hold values from -0.21875 to 0.21875
- w_so: bfloat16 [768, 768], replicated, may hold values from -1.75 to 1.75
- w_cq: bfloat16 [768, 768], replicated, may hold values from -0.21875 to 0.21875
- w_ck: bfloat16 [768, 768], replicated, may hold values from -0.21875 to 0.21875
- w_cv: bfloat16 [768, 768], replicated, may hold values from -0.21875 to 0.21875
- w_co: bfloat16 [768, 768], replicated, may hold values from -6 to 6
- w_in: bfloat16 [768, 3072], replicated, may hold values from -0.21875 to 0.21875
- w_out: bfloat16 [3072, 768], replicated, may hold values from -0.109375 to 0.109375
- gain_self: float32 [768], replicated, may hold values from 0.5 to 1.5
- gain_cross: float32 [768], replicated, may hold values from 0.5 to 1.5
- gain_ffn: float32 [768], replicated, may hold values from 0.5 to 1.5
- cotangent: bfloat16 [32, 128, 768], P(('pb', 'pa')), may hold values from -6 to 6
Outputs:
- out: bfloat16 [32, 128, 768], P(('pb', 'pa'))
- grad_hidden: bfloat16 [32, 128, 768], P(('pb', 'pa'))
- grad_encoder: bfloat16 [32, 4, 384, 768], P('pb', 'pa')
- grad_w_sq: float32 [768, 768], P('pa')
- grad_w_sk: float32 [768, 768], P('pa')
- grad_w_sv: float32 [768, 768], P('pa')
- grad_w_so: float32 [768, 768], P('pa')
- grad_w_cq: float32 [768, 768], P('pa')
- grad_w_ck: float32 [768, 768], P('pa')
- grad_w_cv: float32 [768, 768], P('pa')
- grad_w_co: float32 [768, 768], P('pa')
- grad_w_in: float32 [768, 3072], P('pa')
- grad_w_out: float32 [3072, 768], P('pa')
- grad_gain_self: float32 [768], P('pa')
- grad_gain_cross: float32 [768], P('pa')
- grad_gain_ffn: float32 [768], P('pa')
Inputs may be any that keep to these rules, and one draw needn't show every extreme that they name: Every passage has at least one true token and each question has a passage of exactly 384 true tokens; the lengths of a question sum to 1152.
All inputs are finite; a program needn't handle non-finite values. No bound on the sum of `lengths` on one device may be relied on, other than what follows from the above.
Results may differ from a plain program's by a relative error of at most 0.02.
Values may be sent and summed in bfloat16 or wider, within the bound.
No kernel may reach another device: no remote copies, remote signals or barrier semaphores. Data moves between devices by JAX's collectives and lax.ppermute only.
A program may use at most 192 MiB of HBM per device.

v0:
```python
import functools

import jax
import jax.numpy as jnp
from jax import lax
from jax.experimental import pallas as pl
from jax.experimental.pallas import tpu as pltpu
from jax.sharding import PartitionSpec as P

HEADS = 12
EPS = 1e-06
NEG = -1000000000.0
F32 = jnp.float32
BF = jnp.bfloat16
SLOTS = 8
LANES = 128
EXTRA_ROWS = 16
MIB = 1 << 20


def dot(left, right, left_dim, right_dim, precision=None):
    return lax.dot_general(
        left,
        right,
        (((left_dim,), (right_dim,)), ((), ())),
        precision=precision,
        preferred_element_type=F32,
    )


def nn(left, right):
    return dot(left, right, 1, 0)


def nt(left, right):
    return dot(left, right, 1, 1)


def tn(left, right):
    return dot(left, right, 0, 0)


def low(values):
    return values.astype(BF)


def inverse_rms(values):
    return lax.rsqrt(jnp.mean(values * values, axis=-1, keepdims=True) + EPS)


def norm_back(grad, values, gain):
    inv = inverse_rms(values)
    scaled = gain * grad
    inner = jnp.mean(values * scaled, axis=-1, keepdims=True)
    grad_values = inv * scaled - values * (inv * inv * inv * inner)
    grad_gain = jnp.sum(grad * values * inv, axis=0, keepdims=True)
    return grad_values, grad_gain


def lanes_of(shape):
    return lax.broadcasted_iota(jnp.int32, shape, len(shape) - 1)


def rows_of(shape):
    return lax.broadcasted_iota(jnp.int32, shape, len(shape) - 2)


def ones_where(condition):
    return jnp.where(condition, 1.0, 0.0).astype(BF)


def spread_matrix(width):
    slot, lane = rows_of((LANES, width)), lanes_of((LANES, width))
    return ones_where((slot // SLOTS == lane // (width // HEADS)) & (slot % SLOTS < 3))


def compact_matrix():
    slot, lane = rows_of((LANES, LANES)), lanes_of((LANES, LANES))
    return ones_where((slot // SLOTS == lane // SLOTS) & (slot % SLOTS < 3))


def gather_matrix(width):
    feature, lane = rows_of((width, LANES)), lanes_of((width, LANES))
    return ones_where(feature // (width // HEADS) == lane // SLOTS)


def split_three(values):
    first = low(values).astype(F32)
    rest = values - first
    second = low(rest).astype(F32)
    third = low(rest - second).astype(F32)
    return first, second, third


def in_slots(values, start=0):
    first, second, third = split_three(values)
    slot = lanes_of(values.shape) % SLOTS - start
    return jnp.where(slot == 0, first, jnp.where(slot == 1, second, jnp.where(slot == 2, third, 0.0)))


def head_sums(values, matrix):
    first, second, third = split_three(values)
    return nn(low(first), matrix) + nn(low(second), matrix) + nn(low(third), matrix)


def two_heads(block):
    first = lanes_of(block.shape) < block.shape[1] // 2
    zero = jnp.zeros_like(block)
    return jnp.concatenate([jnp.where(first, block, zero), jnp.where(first, zero, block)], 0)


def fold_heads(block):
    half = block.shape[0] // 2
    lane = lanes_of((half, block.shape[1]))
    return jnp.where(lane < block.shape[1] // 2, block[:half], block[half:])


def pair_of_slots(extra, pair, start, more=None):
    lane = lanes_of(extra.shape)
    slot = lane % SLOTS
    wanted = (slot >= start) & (slot < start + 3)
    halves = [
        jnp.where(wanted & (lane // SLOTS == 2 * pair + i), extra, jnp.zeros_like(extra)) for i in range(2)
    ]
    block = jnp.concatenate(halves, 0)
    return block if more is None else block + more


def last_lane(rows, value):
    return jnp.where(lanes_of((rows, LANES)) == LANES - 1, value, 0.0).astype(BF)


def attend_pair(queries, keys, values, valid=None):
    scores = nt(keys, queries)
    if valid is not None:
        scores = jnp.where(valid, scores, NEG)
    top = jnp.max(scores, axis=0, keepdims=True)
    weights = low(jnp.exp(scores - top))
    both = tn(weights, values)
    split = both.shape[1] - LANES
    mixture = fold_heads(both[:, :split]) * (1.0 / fold_heads(both[:, split:]))
    return mixture, both[:, split:], top


def log_totals(sums, tops):
    tokens = tops[0].shape[1] // 2
    lane = lanes_of((tokens, LANES)) // SLOTS
    found = jnp.ones((tokens, LANES), F32)
    rows = []
    for pair, (both, top) in enumerate(zip(sums, tops)):
        found = jnp.where(lane == 2 * pair, both[:tokens], jnp.where(lane == 2 * pair + 1, both[tokens:], found))
        rows += [jnp.broadcast_to(top[:, :tokens], (SLOTS, tokens)), jnp.broadcast_to(top[:, tokens:], (SLOTS, tokens))]
    rows.append(jnp.zeros((LANES - HEADS * SLOTS, tokens), F32))
    return jnp.transpose(jnp.concatenate(rows, 0)) + jnp.log(found)


def attend_pair_back(queries, keys, values, grad_mix, query_more, key_more, grad_more, value_more, valid=None):
    scaled = two_heads(queries)
    grad_two = two_heads(grad_mix)
    scores = nt(jnp.concatenate([keys, key_more], 1), jnp.concatenate([scaled, query_more], 1))
    probs = jnp.exp(scores)
    if valid is not None:
        probs = jnp.where(valid, probs, 0.0)
    grad_probs = nt(jnp.concatenate([values, value_more], 1), jnp.concatenate([grad_two, grad_more], 1))
    grad_scores = low(probs * grad_probs)
    grad_values = nn(low(probs), grad_two)
    grad_keys = nn(grad_scores, scaled)
    grad_queries = fold_heads(tn(grad_scores, keys))
    return grad_queries, grad_keys, grad_values


def minus_slots(rows, start):
    slot = lanes_of((rows, LANES)) % SLOTS
    return jnp.where((slot >= start) & (slot < start + 3), -1.0, 0.0)


def causal_mask(tokens):
    key = rows_of((tokens, 2 * tokens))
    token = lanes_of((tokens, 2 * tokens))
    return key <= jnp.where(token >= tokens, token - tokens, token)


def call(kernel, name, outs, args, mib, scratch=(), places=None):
    kinds = {"s": pltpu.SMEM, "h": pltpu.HBM, "v": pltpu.VMEM}
    specs = [pl.BlockSpec(memory_space=kinds[letter]) for letter in places]
    return pl.pallas_call(
        kernel,
        out_shape=outs,
        in_specs=specs,
        out_specs=jax.tree.map(lambda _: pl.BlockSpec(memory_space=pltpu.VMEM), outs),
        scratch_shapes=scratch,
        compiler_params=pltpu.CompilerParams(vmem_limit_bytes=mib * MIB),
        cost_estimate=pl.CostEstimate(flops=1000, bytes_accessed=1000, transcendentals=0),
        name=name,
    )(*args)


def shape(*dims):
    return jax.ShapeDtypeStruct(dims, BF)


def shape32(*dims):
    return jax.ShapeDtypeStruct(dims, F32)


def fetch(copies):
    for item in copies:
        item.start()
    return copies


def self_forward_kernel(ids, hidden, cot, gain_self, gain_cross, *refs, chips):
    weights, refs = refs[:5], refs[5:]
    (q_out, k_out, v_out, mixture_out, logs_out, mix_out, after_out, x_cross_out, cross_q_out) = refs[:9]
    early, held, sems = refs[9 : 9 + chips], refs[9 + chips], refs[10 + chips]
    copies = fetch([pltpu.make_async_copy(w, held.at[i], sems.at[i]) for i, w in enumerate(weights)])
    stream = hidden[...].astype(F32)
    tokens, width = stream.shape
    factor = (width // HEADS) ** -0.5
    x_self = low(stream * inverse_rms(stream) * gain_self[...])
    found = []
    for i, out in enumerate((q_out, k_out, v_out)):
        copies[i].wait()
        found.append(low(nn(x_self, held[i])))
        out[...] = found[i]
    queries, keys, values = found
    valid = causal_mask(tokens)
    pair_width = 2 * width // HEADS
    ones = jnp.ones((tokens, LANES), BF)
    mixtures, sums, tops = [], [], []
    for pair in range(HEADS // 2):
        part = slice(pair * pair_width, (pair + 1) * pair_width)
        mixture, both, top = attend_pair(
            two_heads(queries[:, part] * factor), keys[:, part], jnp.concatenate([values[:, part], ones], 1), valid
        )
        mixtures.append(mixture)
        sums.append(both)
        tops.append(top)
    logs_out[...] = log_totals(sums, tops)
    mixture = jnp.concatenate(mixtures, 1)
    mixture_out[...] = mixture
    mix = low(mixture)
    mix_out[...] = mix
    copies[3].wait()
    after_self = stream + nn(mix, held[3])
    after_out[...] = after_self
    x_cross = low(after_self * inverse_rms(after_self) * gain_cross[...])
    x_cross_out[...] = x_cross
    copies[4].wait()
    cross_q_out[...] = low(nn(x_cross, held[4]))
    chip = ids[1]
    for by, out in enumerate(early):
        out[:, width:] = cot[...]
        last = lax.div((chip ^ by) * 4, chips) == 3

        @pl.when(last)
        def _():
            out[:, :width] = mix

        @pl.when(jnp.logical_not(last))
        def _():
            out[:, :width] = x_self


def self_forward(ids, hidden, cot, gain_self, gain_cross, weights, chips):
    tokens, width = hidden.shape
    low_one = shape(tokens, width)
    return call(
        functools.partial(self_forward_kernel, chips=chips),
        "self_forward",
        (low_one, low_one, low_one, shape32(tokens, width), shape32(tokens, LANES), low_one,
         shape32(tokens, width), low_one, low_one) + (shape(tokens, 2 * width),) * chips,
        (ids, hidden, cot, gain_self, gain_cross) + tuple(weights),
        20,
        [pltpu.VMEM((5, width, width), BF), pltpu.SemaphoreType.DMA((5,))],
        "svvvv" + "h" * 5,
    )


def question_of(step, ids, count):
    return lax.rem(ids[0] + count - step, count)


def cross_forward_kernel(ids, lengths, keys, values, *refs):
    count = (len(refs) - 1) // 2
    asked, outs, queries = refs[:count], refs[count : 2 * count], refs[-1]
    step = pl.program_id(0)
    tokens, width = queries.shape
    for index, item in enumerate(asked):

        @pl.when(step == index)
        def _():
            queries[...] = item[...]

    key_count = keys.shape[0]
    factor = (width // HEADS) ** -0.5
    size = (key_count, LANES)
    hidden_key = jnp.where(rows_of(size) < lengths[question_of(step, ids, count)], 0.0, NEG)
    key_more = jnp.where(lanes_of(size) == LANES - 1, hidden_key, 0.0).astype(BF)
    query_more = last_lane(2 * tokens, 1.0)
    ones = jnp.ones(size, BF)
    pair_width = 2 * width // HEADS
    mixtures, sums, tops = [], [], []
    for pair in range(HEADS // 2):
        part = slice(pair * pair_width, (pair + 1) * pair_width)
        mixture, both, top = attend_pair(
            jnp.concatenate([two_heads(queries[:, part] * factor), query_more], 1),
            jnp.concatenate([keys[:, part], key_more], 1),
            jnp.concatenate([values[:, part], ones], 1),
        )
        mixtures.append(low(mixture))
        sums.append(both)
        tops.append(top)
    packed = jnp.concatenate(mixtures + [low(in_slots(log_totals(sums, tops)))], 1)
    for index, out in enumerate(outs):

        @pl.when(step == index)
        def _():
            out[...] = packed


def cross_forward(ids, lengths, asked, keys, values):
    count = len(asked)
    tokens, width = asked[0].shape
    key_spec = pl.BlockSpec((keys.shape[0] // count, width), lambda s, ids, n: (question_of(s, ids, count), 0))
    whole = lambda lanes: pl.BlockSpec((tokens, lanes), lambda s, ids, n: (0, 0))
    return pl.pallas_call(
        cross_forward_kernel,
        grid_spec=pltpu.PrefetchScalarGridSpec(
            num_scalar_prefetch=2,
            grid=(count,),
            in_specs=[key_spec, key_spec] + [whole(width)] * count,
            out_specs=[whole(width + LANES)] * count,
            scratch_shapes=[pltpu.VMEM((tokens, width), BF)],
        ),
        out_shape=[shape(tokens, width + LANES)] * count,
        compiler_params=pltpu.CompilerParams(vmem_limit_bytes=20 * MIB),
        cost_estimate=pl.CostEstimate(flops=1000, bytes_accessed=1000, transcendentals=0),
        name="cross_forward",
    )(ids, lengths, keys, values, *asked)


def feed_forward_kernel(
    ids, after_self, cotangent, x_cross, gain_ffn, w_co_far, w_in_far, w_out_far, *refs, count, chips, chunks
):
    packed, refs = refs[:count], refs[count:]
    result_out, grad_after_out, g_cross_out, send_out, grad_gain_out = refs[:5]
    middle = refs[5 : 5 + chips]
    w_co, w_in, w_out, acts, grad_pres, sems = refs[5 + chips :]
    tokens, width = after_self.shape
    units = w_in.shape[1]
    wide = units // chunks
    first = pltpu.make_async_copy(w_co_far, w_co, sems.at[0])
    first.start()
    copies = []
    for chunk in range(chunks):
        part = pl.ds(chunk * wide, wide)
        copies.append(
            fetch([
                pltpu.make_async_copy(w_in_far.at[:, part], w_in.at[:, part], sems.at[1 + 2 * chunk]),
                pltpu.make_async_copy(w_out_far.at[part], w_out.at[part], sems.at[2 + 2 * chunk]),
            ])
        )
    compact, spread = compact_matrix(), spread_matrix(width)
    logs = [nn(part[:, width:], compact) for part in packed]
    top = functools.reduce(jnp.maximum, logs)
    log_total = top + jnp.log(sum(jnp.exp(item - top) for item in logs))
    mixture = sum(
        nn(low(in_slots(jnp.exp(item - log_total))), spread) * part[:, :width].astype(F32)
        for item, part in zip(logs, packed)
    )
    mix = low(mixture)
    first.wait()
    after_cross = after_self[...] + nn(mix, w_co[...])
    x_ffn = low(after_cross * inverse_rms(after_cross) * gain_ffn[...])
    grad_low = cotangent[...]
    result = after_cross
    grad_x = jnp.zeros((tokens, width), F32)
    slope = (2.0 / 3.141592653589793) ** 0.5
    span = units // chips
    piece = units // (count * chips)
    for chunk in range(chunks):
        part = slice(chunk * wide, (chunk + 1) * wide)
        for item in copies[chunk]:
            item.wait()
        pre = nn(x_ffn, w_in[:, part])
        square = pre * pre
        bent = jnp.tanh(pre * (slope + (0.044715 * slope) * square))
        act = low(0.5 * pre * (1.0 + bent))
        result = result + nn(act, w_out[part, :])
        grad_act = nt(grad_low, w_out[part, :])
        bend = 0.5 * (1.0 + bent) + 0.5 * pre * (1.0 - bent * bent) * (slope + (3 * 0.044715 * slope) * square)
        grad_pre = low(grad_act * bend)
        grad_x = grad_x + nt(grad_pre, w_in[:, part])
        for at in range(0, wide, piece):
            which = (chunk * wide + at) // piece
            slot = which // chips * piece
            acts[which % chips, :, slot : slot + piece] = act[:, at : at + piece]
        for at in range(0, wide, span):
            grad_pres[(chunk * wide + at) // span] = grad_pre[:, at : at + span]
    result_out[...] = low(result)
    grad_values, grad_gain = norm_back(grad_x, after_cross, gain_ffn[...])
    grad_gain_out[...] = grad_gain
    grad_after = grad_low.astype(F32) + grad_values
    grad_after_out[...] = grad_after
    g_cross = low(grad_after)
    g_cross_out[...] = g_cross
    grad_mix = low(nt(g_cross, w_co[...]))
    delta = head_sums(grad_mix.astype(F32) * mixture, gather_matrix(width))
    send_out[:, :width] = grad_mix
    send_out[:, width:] = low(in_slots(log_total) + in_slots(delta, 3))
    chip = ids[1]
    for by, out in enumerate(middle):
        index = chip ^ by
        out[:, :width] = x_ffn
        out[:, 2 * width : 2 * width + span] = acts[index]
        out[:, 2 * width + span :] = grad_pres[index]
        early = lax.div(index * 2, chips) == 0

        @pl.when(early)
        def _():
            out[:, width : 2 * width] = mix

        @pl.when(jnp.logical_not(early))
        def _():
            out[:, width : 2 * width] = x_cross[...]


def feed_forward(ids, after_self, cotangent, x_cross, gain_ffn, w_co, w_in, w_out, packed, chips):
    tokens, width = after_self.shape
    units = w_in.shape[1]
    span, chunks = units // chips, 4
    return call(
        functools.partial(feed_forward_kernel, count=len(packed), chips=chips, chunks=chunks),
        "feed_forward",
        (shape(tokens, width), shape32(tokens, width), shape(tokens, width), shape(tokens, width + LANES),
         shape32(1, width)) + (shape(tokens, 2 * width + 2 * span),) * chips,
        (ids, after_self, cotangent, x_cross, gain_ffn, w_co, w_in, w_out) + tuple(packed),
        32,
        [
            pltpu.VMEM(w_co.shape, BF),
            pltpu.VMEM(w_in.shape, BF),
            pltpu.VMEM(w_out.shape, BF),
            pltpu.VMEM((chips, tokens, span), BF),
            pltpu.VMEM((chips, tokens, span), BF),
            pltpu.SemaphoreType.DMA((1 + 2 * chunks,)),
        ],
        "svvvvhhh" + "v" * len(packed),
    )


def cross_backward_kernel(ids, lengths, keys, values, *refs):
    count = (len(refs) - 4) // 3
    asked, given = refs[:count], refs[count : 2 * count]
    grad_keys, grad_values = refs[2 * count : 2 * count + 2]
    outs = refs[2 * count + 2 : 3 * count + 2]
    queries, grads = refs[3 * count + 2 :]
    step = pl.program_id(0)
    tokens, width = queries.shape
    for index in range(count):

        @pl.when(step == index)
        def _():
            queries[...] = asked[index][...]
            grads[...] = given[index][...]

    key_count = keys.shape[0]
    factor = (width // HEADS) ** -0.5
    size = (key_count, LANES)
    hidden_key = jnp.where(rows_of(size) < lengths[question_of(step, ids, count)], 0.0, NEG)
    key_more = jnp.where(lanes_of(size) == LANES - 1, hidden_key, minus_slots(key_count, 0)).astype(BF)
    value_more = minus_slots(key_count, 3).astype(BF)
    extra = grads[:, width:]
    one = last_lane(2 * tokens, 1.0)
    pair_width = 2 * width // HEADS
    found = []
    for pair in range(HEADS // 2):
        part = slice(pair * pair_width, (pair + 1) * pair_width)
        grad_q, grad_k, grad_v = attend_pair_back(
            queries[:, part] * factor, keys[:, part], values[:, part], grads[:, part],
            pair_of_slots(extra, pair, 0, one), key_more, pair_of_slots(extra, pair, 3), value_more,
        )
        found.append(low(grad_q * factor))
        grad_keys[:, part] = low(grad_k)
        grad_values[:, part] = low(grad_v)
    grad_queries = jnp.concatenate(found, 1)
    for index, out in enumerate(outs):

        @pl.when(step == index)
        def _():
            out[...] = grad_queries


def cross_backward(ids, lengths, asked, given, keys, values):
    count = len(asked)
    tokens, width = asked[0].shape
    key_spec = pl.BlockSpec((keys.shape[0] // count, width), lambda s, ids, n: (question_of(s, ids, count), 0))
    whole = lambda lanes: pl.BlockSpec((tokens, lanes), lambda s, ids, n: (0, 0))
    return pl.pallas_call(
        cross_backward_kernel,
        grid_spec=pltpu.PrefetchScalarGridSpec(
            num_scalar_prefetch=2,
            grid=(count,),
            in_specs=[key_spec, key_spec] + [whole(width)] * count + [whole(width + LANES)] * count,
            out_specs=[key_spec, key_spec] + [whole(width)] * count,
            scratch_shapes=[pltpu.VMEM((tokens, width), BF), pltpu.VMEM((tokens, width + LANES), BF)],
        ),
        out_shape=[jax.ShapeDtypeStruct(keys.shape, BF)] * 2 + [shape(tokens, width)] * count,
        compiler_params=pltpu.CompilerParams(vmem_limit_bytes=24 * MIB),
        cost_estimate=pl.CostEstimate(flops=1000, bytes_accessed=1000, transcendentals=0),
        name="cross_backward",
    )(ids, lengths, keys, values, *asked, *given)


def gain_block(gains, four, width_out):
    count = gains.shape[1] // four
    high = low(gains).astype(F32)
    rows = [part[i : i + 1, v * four : (v + 1) * four] for part in (high, gains - high) for i in range(3) for v in range(count)]
    block = jnp.concatenate(rows + [jnp.zeros((EXTRA_ROWS - len(rows), four), F32)], 0)
    return low(jnp.concatenate([block, jnp.zeros((EXTRA_ROWS, width_out - four), F32)], 1))


def gain_values(block, four, width):
    count = width // four
    rows = []
    for i in range(3):
        pieces = [
            block[i * count + v : i * count + v + 1, :four] + block[(3 + i) * count + v : (3 + i) * count + v + 1, :four]
            for v in range(count)
        ]
        rows.append(jnp.concatenate(pieces, 1))
    return jnp.concatenate(rows, 0)


def self_backward_kernel(
    ids, grad_after_cross, after_self, hidden, gain_self, gain_cross, grad_gain_ffn, g_cross,
    self_q, self_k, self_v, mixture, logs, *refs, count, chips
):
    weights, partial, refs = refs[:5], refs[5 : 5 + count], refs[5 + count :]
    hidden_out, late = refs[0], refs[1 : 1 + chips]
    held, fours, twos, sems = refs[1 + chips :]
    copies = fetch([pltpu.make_async_copy(w, held.at[i], sems.at[i]) for i, w in enumerate(weights)])
    tokens, width = after_self.shape
    factor = (width // HEADS) ** -0.5
    four, two = 4 * width // chips, 2 * width // chips
    grad_cq = low(sum(item[...].astype(F32) for item in partial))
    copies[0].wait()
    grad_values, grad_gain_cross = norm_back(nt(grad_cq, held[0]), after_self[...], gain_cross[...])
    grad_after = grad_after_cross[...] + grad_values
    g_self = low(grad_after)
    copies[1].wait()
    grad_mix = low(nt(g_self, held[1]))
    delta = head_sums(grad_mix.astype(F32) * mixture[...], gather_matrix(width))
    extra = low(in_slots(logs[...]) + in_slots(delta, 3))
    valid = causal_mask(tokens)
    key_more = minus_slots(tokens, 0).astype(BF)
    value_more = minus_slots(tokens, 3).astype(BF)
    pair_width = 2 * width // HEADS
    found = []
    for pair in range(HEADS // 2):
        part = slice(pair * pair_width, (pair + 1) * pair_width)
        grad_q, grad_k, grad_v = attend_pair_back(
            self_q[:, part] * factor, self_k[:, part], self_v[:, part], grad_mix[:, part],
            pair_of_slots(extra, pair, 0), key_more, pair_of_slots(extra, pair, 3), value_more, valid,
        )
        found.append((low(grad_q * factor), low(grad_k), low(grad_v)))
    grads = [jnp.concatenate([item[i] for item in found], 1) for i in range(3)]
    grad_x = jnp.zeros((tokens, width), F32)
    for i in range(3):
        copies[2 + i].wait()
        grad_x = grad_x + nt(grads[i], held[2 + i])
    grad_values, grad_gain_self = norm_back(grad_x, hidden[...].astype(F32), gain_self[...])
    hidden_out[...] = low(grad_after + grad_values)
    gains = jnp.concatenate([grad_gain_self, grad_gain_cross, grad_gain_ffn[...]], 0)
    block = gain_block(gains, four, four + two)
    for i, item in enumerate(grads + [g_self]):
        for v in range(width // four):
            fours[i * (width // four) + v] = item[:, v * four : (v + 1) * four]
    for i, item in enumerate((g_cross[...], grad_cq)):
        for v in range(width // two):
            twos[i * (width // two) + v] = item[:, v * two : (v + 1) * two]
    chip = ids[1]
    for by, out in enumerate(late):
        out[:tokens, :four] = fours[chip ^ by]
        out[:tokens, four:] = twos[chip ^ by]
        out[tokens:] = block


def self_backward(ids, first, weights, partial, chips):
    tokens, width = first[1].shape
    four, two = 4 * width // chips, 2 * width // chips
    return call(
        functools.partial(self_backward_kernel, count=len(partial), chips=chips),
        "self_backward",
        (shape(tokens, width),) + (shape(tokens + EXTRA_ROWS, four + two),) * chips,
        (ids,) + tuple(first) + tuple(weights) + tuple(partial),
        24,
        [
            pltpu.VMEM((5, width, width), BF),
            pltpu.VMEM((chips, tokens, four), BF),
            pltpu.VMEM((chips, tokens, two), BF),
            pltpu.SemaphoreType.DMA((5,)),
        ],
        "s" + "v" * len(first) + "h" * 5 + "v" * len(partial),
    )


def stacked(refs, rows, lanes):
    return jnp.concatenate([item[rows, lanes] for item in refs], 0)


def hand_out(ids, held, keep, give):
    core = ids[2]
    keep[...] = held[core]
    give[...] = held[1 - core]


def ffn_grads_kernel(ids, *refs, chips):
    early, middle, (keep, give, held) = refs[:chips], refs[chips : 2 * chips], refs[2 * chips :]
    _, ring, half, both = held.shape
    span = both // 2
    width = early[0].shape[1] // 2
    every = slice(None)
    grad_in = low(
        tn(stacked(middle, every, slice(0, width)), stacked(middle, every, slice(2 * width + span, 2 * width + 2 * span)))
    )
    for z in range(ring):
        for c in range(2):
            at = (2 * z + c) * half
            held[c, z, :, :span] = grad_in[at : at + half]
    grad_out = low(
        tn(stacked(middle, every, slice(2 * width, 2 * width + span)), stacked(early, every, slice(width, 2 * width)))
    )
    few = span // (2 * ring)
    for z in range(ring):
        for c in range(2):
            at = (2 * z + c) * few
            block = grad_out[at : at + few]
            held[c, z, :, span:] = jnp.concatenate([block[:, v : v + span] for v in range(0, width, span)], 0)
    hand_out(ids, held, keep, give)


def ffn_grads(ids, early, middle, ring, units):
    chips = len(early)
    width = early[0].shape[1] // 2
    part = (ring, width // (2 * ring), 2 * units // chips)
    return call(
        functools.partial(ffn_grads_kernel, chips=chips), "ffn_grads", (shape(*part),) * 2,
        (ids,) + tuple(early) + tuple(middle), 36, [pltpu.VMEM((2,) + part, BF)], "s" + "v" * (2 * chips),
    )


def key_grads_kernel(ids, encoder, grad_keys, grad_values, keep, give, held):
    _, ring, half, both = held.shape
    width = both // 2
    for i, item in enumerate((grad_keys, grad_values)):
        grad = low(tn(encoder[...], item[...]))
        for z in range(ring):
            for c in range(2):
                at = (2 * z + c) * half
                held[c, z, :, i * width : (i + 1) * width] = grad[at : at + half]
    hand_out(ids, held, keep, give)


def key_grads(ids, encoder, grad_keys, grad_values, ring):
    width = encoder.shape[1]
    part = (ring, width // (2 * ring), 2 * width)
    return call(
        key_grads_kernel, "key_grads", (shape(*part),) * 2, (ids, encoder, grad_keys, grad_values), 36,
        [pltpu.VMEM((2,) + part, BF)], "svvv",
    )


def key_sum_kernel(ids, keep, came, *refs):
    outs, held = refs[:-1], refs[-1]
    chips, two = held.shape[0], held.shape[3]
    summed = low(keep[...].astype(F32) + came[...].astype(F32))
    for j in range(chips):
        held[j] = summed[:, :, j * two : (j + 1) * two]
    for by, out in enumerate(outs):
        out[...] = held[ids[1] ^ by]


def key_sum(ids, keep, came, chips):
    ring, half, both = keep.shape
    part = (ring, half, both // chips)
    return call(
        key_sum_kernel, "key_sum", (shape(*part),) * chips, (ids, keep, came), 20, [pltpu.VMEM((chips,) + part, BF)], "svv"
    )


def first_sum_kernel(ids, keep, came, *refs, chips):
    parts, outs = refs[:chips], refs[chips:]
    ring = len(outs)
    wide = keep.shape[2]
    for by, out in enumerate(outs):
        z = lax.rem(ids[0] + by, ring)
        out[:, :wide] = low(keep[z].astype(F32) + came[z].astype(F32))
        out[:, wide:] = low(sum(item[z].astype(F32) for item in parts))


def first_sum(ids, keep, came, parts):
    ring, half, wide = keep.shape
    out = shape(half, wide + parts[0].shape[2])
    return call(
        functools.partial(first_sum_kernel, chips=len(parts)), "first_sum", (out,) * ring,
        (ids, keep, came) + tuple(parts), 20, (), "svv" + "v" * len(parts),
    )


def tail_grads_kernel(ids, *refs, chips):
    early, middle, late = refs[:chips], refs[chips : 2 * chips], refs[2 * chips : 3 * chips]
    keep, give, held = refs[3 * chips :]
    _, ring, more, both = held.shape
    half = more - EXTRA_ROWS
    four = both // 3 * 2
    width = early[0].shape[1] // 2
    tokens = early[0].shape[0]
    every, rows = slice(None), slice(0, tokens)
    grads = (
        (low(tn(stacked(early, every, slice(0, width)), stacked(late, rows, slice(0, four)))), slice(0, four)),
        (low(tn(stacked(middle, every, slice(width, 2 * width)), stacked(late, rows, slice(four, both)))), slice(four, both)),
    )
    gains = sum(gain_values(item[tokens:].astype(F32), four, width) for item in late)
    block = gain_block(gains, four, both)
    for z in range(ring):
        for c in range(2):
            at = (2 * z + c) * half
            for grad, lanes in grads:
                held[c, z, :half, lanes] = grad[at : at + half]
            held[c, z, half:, :] = block
    hand_out(ids, held, keep, give)


def tail_grads(ids, early, middle, late, ring):
    chips = len(early)
    width = early[0].shape[1] // 2
    part = (ring, width // (2 * ring) + EXTRA_ROWS, late[0].shape[1])
    return call(
        functools.partial(tail_grads_kernel, chips=chips), "tail_grads", (shape(*part),) * 2,
        (ids,) + tuple(early) + tuple(middle) + tuple(late), 36, [pltpu.VMEM((2,) + part, BF)], "s" + "v" * (3 * chips),
    )


def tail_sum_kernel(ids, keep, came, *outs):
    ring = len(outs)
    half = keep.shape[1] - EXTRA_ROWS
    four = keep.shape[2] // 3 * 2
    width = half * 2 * ring
    gains = gain_values(keep[0, half:].astype(F32), four, width) + gain_values(came[0, half:].astype(F32), four, width)
    block = gain_block(gains, four, keep.shape[2])
    for by, out in enumerate(outs):
        z = lax.rem(ids[0] + by, ring)
        out[:half] = low(keep[z, :half].astype(F32) + came[z, :half].astype(F32))
        out[half:] = block


def tail_sum(ids, keep, came):
    ring, more, both = keep.shape
    return call(tail_sum_kernel, "tail_sum", (shape(more, both),) * ring, (ids, keep, came), 20, (), "svv")


def ring_sum_kernel(*refs):
    refs[-1][...] = low(sum(item[...].astype(F32) for item in refs[:-1]))


def ring_sum(parts):
    return call(ring_sum_kernel, "ring_sum", shape(*parts[0].shape), tuple(parts), 16, (), "v" * len(parts))


def last_sum_kernel(ids, *refs):
    parts, (out, gains_out, held) = refs[:-3], refs[-3:]
    half, both = out.shape
    ring, _, rows = held.shape
    four = both // 3 * 2
    out[...] = low(sum(item[:half].astype(F32) for item in parts))
    gains = sum(gain_values(item[half:].astype(F32), four, ring * rows) for item in parts)
    for z in range(ring):
        held[z] = gains[:, z * rows : (z + 1) * rows]
    gains_out[...] = held[ids[0]]


def last_sum(ids, parts, rows):
    more, both = parts[0].shape
    return call(
        last_sum_kernel, "last_sum", (shape(more - EXTRA_ROWS, both), shape32(3, rows)), (ids,) + tuple(parts), 16,
        [pltpu.VMEM((len(parts), 3, rows), F32)], "s" + "v" * len(parts),
    )


def place_pieces(ids, own, other, held):
    for by, (mine, theirs) in enumerate(zip(own, other)):
        held[ids[1] ^ by, ids[2]] = mine[...]
        held[ids[1] ^ by, 1 - ids[2]] = theirs[...]


def first_out_kernel(ids, *refs, chips, span):
    own, other, (in_out, out_out, ck_out, cv_out, held) = refs[:chips], refs[chips : 2 * chips], refs[2 * chips :]
    place_pieces(ids, own, other, held)
    half, wide = held.shape[2:]
    two = wide - 2 * span
    width = out_out.shape[1]
    few = half * span // width
    for j in range(chips):
        for c in range(2):
            rows = slice(c * half, (c + 1) * half)
            in_out[rows, j * span : (j + 1) * span] = held[j, c, :, :span].astype(F32)
            for v in range(width // span):
                at = (2 * j + c) * few
                out_out[at : at + few, v * span : (v + 1) * span] = held[
                    j, c, v * few : (v + 1) * few, span : 2 * span
                ].astype(F32)
            out = (ck_out, cv_out)[j * 2 // chips]
            at = j % (chips // 2) * two
            out[rows, at : at + two] = held[j, c, :, 2 * span :].astype(F32)


def first_out(ids, own, other, units, width):
    chips = len(own)
    half, wide = own[0].shape
    span = units // chips
    rows = 2 * half
    return call(
        functools.partial(first_out_kernel, chips=chips, span=span), "first_out",
        (shape32(rows, units), shape32(rows * units // width, width), shape32(rows, width), shape32(rows, width)),
        (ids,) + tuple(own) + tuple(other), 28, [pltpu.VMEM((chips, 2, half, wide), BF)], "s" + "v" * (2 * chips),
    )


def last_out_kernel(ids, *refs, chips):
    own, other, outs, held = refs[:chips], refs[chips : 2 * chips], refs[2 * chips : -1], refs[-1]
    place_pieces(ids, own, other, held)
    half, both = held.shape[2:]
    four, two = both // 3 * 2, both // 3
    for j in range(chips):
        for c in range(2):
            rows = slice(c * half, (c + 1) * half)
            at = j % (chips // 4) * four
            outs[j * 4 // chips][rows, at : at + four] = held[j, c, :, :four].astype(F32)
            at = j % (chips // 2) * two
            outs[4 + j * 2 // chips][rows, at : at + two] = held[j, c, :, four:].astype(F32)


def last_out(ids, own, other, width):
    chips = len(own)
    half, both = own[0].shape
    return call(
        functools.partial(last_out_kernel, chips=chips), "last_out", (shape32(2 * half, width),) * 6,
        (ids,) + tuple(own) + tuple(other), 28, [pltpu.VMEM((chips, 2, half, both), BF)], "s" + "v" * (2 * chips),
    )


def swap(values, axis, by):
    peers = lax.axis_size(axis)
    return lax.ppermute(values, axis, [(i, i ^ by) for i in range(peers)])


def shift(values, axis, by):
    peers = lax.axis_size(axis)
    return lax.ppermute(values, axis, [(i, (i + by) % peers) for i in range(peers)])


def over_chips(blocks):
    return [blocks[0]] + [swap(item, "pb", 2 * by) for by, item in enumerate(blocks) if by]


def over_ring(blocks, sign=1):
    return [blocks[0]] + [shift(item, "pa", sign * by) for by, item in enumerate(blocks) if by]


def over_core(blocks):
    return [swap(item, "pb", 1) for item in blocks]


def body(
    hidden, encoder, lengths, w_sq, w_sk, w_sv, w_so, w_cq, w_ck, w_cv, w_co, w_in, w_out,
    gain_self, gain_cross, gain_ffn, cotangent,
):
    _, tokens, width = hidden.shape
    questions, _, passage_len, _ = encoder.shape
    units = w_in.shape[1]
    ring = lax.axis_size("pa")
    chips = lax.axis_size("pb") // 2
    place, lane = lax.axis_index("pa"), lax.axis_index("pb")
    ids = jnp.stack([place, lane >> 1, lane & 1]).astype(jnp.int32)
    gain_self, gain_cross, gain_ffn = (gain.reshape(1, width) for gain in (gain_self, gain_cross, gain_ffn))
    true_len = lengths.reshape(questions)
    hidden2 = hidden.reshape(tokens, width)
    cot = cotangent.reshape(tokens, width)
    enc = encoder.reshape(questions * passage_len, width)

    found = self_forward(ids, hidden2, cot, gain_self, gain_cross, (w_sq, w_sk, w_sv, w_so, w_cq), chips)
    self_q, self_k, self_v, mixture, logs, _, after_self, x_cross, cross_q = found[:9]
    asked = over_ring([cross_q] * ring)
    early = over_chips(found[9:])
    keys = low(nn(enc, w_ck))
    values = low(nn(enc, w_cv))
    packed = over_ring(cross_forward(ids, true_len, asked, keys, values), -1)
    found = feed_forward(ids, after_self, cot, x_cross, gain_ffn, w_co, w_in, w_out, packed, chips)
    result, grad_after_cross, g_cross, sent, grad_gain_ffn = found[:5]
    given = over_ring([sent] * ring)
    middle = over_chips(found[5:])
    found = cross_backward(ids, true_len, asked, given, keys, values)
    grad_keys, grad_values = found[:2]
    partial = over_ring(found[2:], -1)
    keep, give = key_grads(ids, enc, grad_keys, grad_values, ring)
    key_parts = over_chips(key_sum(ids, keep, swap(give, "pb", 1), chips))
    keep, give = ffn_grads(ids, early, middle, ring, units)
    first = ring_sum(over_ring(first_sum(ids, keep, swap(give, "pb", 1), key_parts)))
    first = over_chips([first] * chips)
    grad_in, grad_out, grad_ck, grad_cv = first_out(ids, first, over_core(first), units, width)
    grad_encoder = low(nt(grad_keys, w_ck) + nt(grad_values, w_cv)).reshape(encoder.shape)
    found = self_backward(
        ids,
        (grad_after_cross, after_self, hidden2, gain_self, gain_cross, grad_gain_ffn, g_cross,
         self_q, self_k, self_v, mixture, logs),
        (w_cq, w_so, w_sq, w_sk, w_sv),
        partial,
        chips,
    )
    grad_hidden = found[0]
    late = over_chips(found[1:])
    keep, give = tail_grads(ids, early, middle, late, ring)
    last, gains = last_sum(ids, over_ring(tail_sum(ids, keep, swap(give, "pb", 1))), width // ring)
    last = over_chips([last] * chips)
    grad_sq, grad_sk, grad_sv, grad_so, grad_co, grad_cq = last_out(ids, last, over_core(last), width)
    return (
        result.reshape(hidden.shape),
        grad_hidden.reshape(hidden.shape),
        grad_encoder,
        grad_sq,
        grad_sk,
        grad_sv,
        grad_so,
        grad_cq,
        grad_ck,
        grad_cv,
        grad_co,
        grad_in,
        grad_out,
        gains[0],
        gains[1],
        gains[2],
    )


def solution(mesh):
    split = P(("pb", "pa"), None, None)
    passages = P("pb", "pa", None, None)
    return jax.shard_map(
        body,
        mesh=mesh,
        in_specs=(split, passages, P("pb", "pa")) + (P(),) * 13 + (split,),
        out_specs=(split, split, passages) + (P("pa", None),) * 10 + (P("pa"),) * 3,
        check_vma=False,
    )
```

profile of v0, /device:TPU:9, one launch (start us, length us, event | category | flops | bytes accessed | tf_op | source)
XLA Modules:
  0.0 284.6 jit_solution(14333583694966966980)
XLA Ops:
  10.4 5.8 %self_forward.1 = (bf16[128,768]{1,0:T(8,128)(2,1)S(1)}, bf16[128,768]{1,0:T(8,128)(2,1)S(1)}, bf16[128,768]{1,0:T(8,128)(2,1)S(1)}, f32[128,768]{1,0:T(8,128)S(...) custom-call(s32[3]{0:T(128)S(1)} %pad_add_fusion.ids, ...), custom_call_target="tpu_custom_call" | custom-call | flops 1000 | bytes 1000 | tf_op jit(solution)/shard_map/self_forward/pallas_call | solution.py:186
  16.4 2.5 collective-permute-start.1
  18.9 2.2 collective-permute-start
  21.1 2.0 convolution_convert_fusion.values
  23.2 2.0 convolution_convert_fusion.1.keys
  25.3 5.9 %collective-permute-done.1.refs_2_ = bf16[128,768]{1,0:T(8,128)(2,1)S(1)} collective-permute-done((bf16[128,768]{1,0:T(8,128)(2,1)S(1)}, bf16[128,768]{1,0:T(8,128)(2,1)S(1)}, u32[]{:S(2)}, u32[]{:S(2)}) %collective-permute-start.1) | collective-permute-done | bytes 196640 | tf_op jit(solution)/shard_map/ppermute | solution.py:860
  31.2 4.2 %collective-permute-done.refs_1_ = bf16[128,768]{1,0:T(8,128)(2,1)S(1)} collective-permute-done((bf16[128,768]{1,0:T(8,128)(2,1)S(1)}, bf16[128,768]{1,0:T(8,128)(2,1)S(1)}, u32[]{:S(2)}, u32[]{:S(2)}) %collective-permute-start) | collective-permute-done | bytes 196640 | tf_op jit(solution)/shard_map/ppermute | solution.py:860
  35.4 6.8 %cross_forward.1 = (bf16[128,896]{1,0:T(8,128)(2,1)S(1)}, bf16[128,896]{1,0:T(8,128)(2,1)S(1)}, bf16[128,896]{1,0:T(8,128)(2,1)S(1)}, bf16[128,896]{1,0:T(8,128)(2,1)S(1)}) custom-call(s32[3]{0:T(128)S(1)} %pad_add_fusion.ids, s32[4]{0:T(128)S(1)} %bitcast.34, bf16[1536,768]{1,0:T(8,128)(2,1)S(1)} %convolution_convert_fusion.1.keys, ...), custom_call_target="tpu_custom_call" | custom-call | flops 1000 | bytes 1000 | tf_op jit(solution)/shard_map/cross_forward/pallas_call | solution.py:327
  43.1 2.6 collective-permute-start.4
  45.7 3.4 %collective-permute-done.3.refs_1_ = bf16[128,896]{1,0:T(8,128)(2,1)S(1)} collective-permute-done((bf16[128,896]{1,0:T(8,128)(2,1)S(1)}, bf16[128,896]{1,0:T(8,128)(2,1)S(1)}, u32[]{:S(2)}, u32[]{:S(2)}) %collective-permute-start.3) | collective-permute-done | bytes 229408 | tf_op jit(solution)/shard_map/ppermute | solution.py:860
  49.1 8.9 %collective-permute-done.4.refs_2_ = bf16[128,896]{1,0:T(8,128)(2,1)S(1)} collective-permute-done((bf16[128,896]{1,0:T(8,128)(2,1)S(1)}, bf16[128,896]{1,0:T(8,128)(2,1)S(1)}, u32[]{:S(2)}, u32[]{:S(2)}) %collective-permute-start.4) | collective-permute-done | bytes 229408 | tf_op jit(solution)/shard_map/ppermute | solution.py:860
  58.0 4.9 %collective-permute-done.5.refs_3_ = bf16[128,896]{1,0:T(8,128)(2,1)S(1)} collective-permute-done((bf16[128,896]{1,0:T(8,128)(2,1)S(1)}, bf16[128,896]{1,0:T(8,128)(2,1)S(1)}, u32[]{:S(2)}, u32[]{:S(2)}) %collective-permute-start.5) | collective-permute-done | bytes 229408 | tf_op jit(solution)/shard_map/ppermute | solution.py:860
  63.0 11.2 %feed_forward.1 = (bf16[128,768]{1,0:T(8,128)(2,1)}, f32[128,768]{1,0:T(8,128)S(1)}, bf16[128,768]{1,0:T(8,128)(2,1)S(1)}, bf16[128,896]{1,0:T(8,128)(2,1)S(1)},...) custom-call(s32[3]{0:T(128)S(1)} %pad_add_fusion.ids, ...), custom_call_target="tpu_custom_call" | custom-call | flops 1000 | bytes 1000 | tf_op jit(solution)/shard_map/feed_forward/pallas_call | solution.py:186
  75.7 2.2 collective-permute-start.8
  83.4 9.3 %collective-permute-done.7.refs_6_ = bf16[128,896]{1,0:T(8,128)(2,1)S(1)} collective-permute-done((bf16[128,896]{1,0:T(8,128)(2,1)S(1)}, bf16[128,896]{1,0:T(8,128)(2,1)S(1)}, u32[]{:S(2)}, u32[]{:S(2)}) %collective-permute-start.7) | collective-permute-done | bytes 229408 | tf_op jit(solution)/shard_map/ppermute | solution.py:860
  92.8 4.9 %collective-permute-done.6.refs_5_ = bf16[128,896]{1,0:T(8,128)(2,1)S(1)} collective-permute-done((bf16[128,896]{1,0:T(8,128)(2,1)S(1)}, bf16[128,896]{1,0:T(8,128)(2,1)S(1)}, u32[]{:S(2)}, u32[]{:S(2)}) %collective-permute-start.6) | collective-permute-done | bytes 229408 | tf_op jit(solution)/shard_map/ppermute | solution.py:860
  97.7 9.8 %cross_backward.1 = (bf16[1536,768]{1,0:T(8,128)(2,1)S(1)}, bf16[1536,768]{1,0:T(8,128)(2,1)S(1)}, bf16[128,768]{1,0:T(8,128)(2,1)S(1)}, bf16[128,768]{1,0:T(8,1...) custom-call(s32[3]{0:T(128)S(1)} %pad_add_fusion.ids, s32[4]{0:T(128)S(1)} %bitcast.35, ...), custom_call_target="tpu_custom_call" | custom-call | flops 1000 | bytes 1000 | tf_op jit(solution)/shard_map/cross_backward/pallas_call | solution.py:499
  112.1 2.5 collective-permute-done.9.refs_6_
  115.8 6.2 %collective-permute-done.10.refs_7_ = bf16[128,768]{1,0:T(8,128)(2,1)S(1)} collective-permute-done((bf16[128,768]{1,0:T(8,128)(2,1)S(1)}, bf16[128,768]{1,0:T(8,128)(2,1)S(1)}, u32[]{:S(2)}, u32[]{:S(2)}) %collective-permute-start.10) | collective-permute-done | bytes 196640 | tf_op jit(solution)/shard_map/ppermute | solution.py:860
  122.0 2.2 collective-permute-start.17
  124.2 2.1 collective-permute-done.11.refs_8_
  126.2 2.2 collective-permute-start.14
  132.2 8.0 %self_backward.1 = (bf16[128,768]{1,0:T(8,128)(2,1)}, bf16[144,1152]{1,0:T(8,128)(2,1)S(1)}, bf16[144,1152]{1,0:T(8,128)(2,1)S(1)}, bf16[144,1152]{1,0:T(8,128)(2,1)S(1)}, bf16[144,1152]{1,0:T(8,128)(2,1)S(1)}) custom-call(s32[3]{0:T(128)S(1)} %pad_add_fusion.ids, f32[128,768]{1,0:T(8,128)S(1)} %get-tuple-element.90.grad_after_cross, ...), custom_call_target="tpu_custom_call" | custom-call | flops 1000 | bytes 1000 | tf_op jit(solution)/shard_map/self_backward/pallas_call | solution.py:186
  140.6 14.7 %collective-permute-done.14.refs_3_ = bf16[128,1536]{1,0:T(8,128)(2,1)S(1)} collective-permute-done((bf16[128,1536]{1,0:T(8,128)(2,1)}, bf16[128,1536]{1,0:T(8,128)(2,1)S(1)}, u32[]{:S(2)}, u32[]{:S(2)}) %collective-permute-start.14) | collective-permute-done | bytes 393248 | tf_op jit(solution)/shard_map/ppermute | solution.py:855
  155.5 5.9 %collective-permute-done.18.refs_9_ = bf16[144,1152]{1,0:T(8,128)(2,1)S(1)} collective-permute-done((bf16[144,1152]{1,0:T(8,128)(2,1)S(1)}, bf16[144,1152]{1,0:T(8,128)(2,1)S(1)}, u32[]{:S(2)}, u32[]{:S(2)}) %collective-permute-start.18) | collective-permute-done | bytes 331808 | tf_op jit(solution)/shard_map/ppermute | solution.py:855
  161.5 2.1 collective-permute-start.20
  164.1 5.6 %collective-permute-done.20.refs_11_ = bf16[144,1152]{1,0:T(8,128)(2,1)S(1)} collective-permute-done((bf16[144,1152]{1,0:T(8,128)(2,1)S(1)}, bf16[144,1152]{1,0:T(8,128)(2,1)S(1)}, u32[]{:S(2)}, u32[]{:S(2)}) %collective-permute-start.20) | collective-permute-done | bytes 331808 | tf_op jit(solution)/shard_map/ppermute | solution.py:855
  171.6 4.7 %collective-permute-start.21 = (bf16[4,112,1152]{2,1,0:T(8,128)(2,1)S(1)}, bf16[4,112,1152]{2,1,0:T(8,128)(2,1)S(1)}, u32[]{:S(2)}, u32[]{:S(2)}) collective-permute-start(bf16[4,112,1152]{2,1,0:T(8,128)(2,1)S(1)} %get-tuple-element.119), channel_id=1, source_target_pairs={{0,4},{4,0},{8,12},{12,8},{16,20},{20,16},{24,28},{28,24},{1,5},{5... | collective-permute-start | bytes 3096584 | tf_op jit(solution)/shard_map/ppermute | solution.py:855
  176.3 4.6 %key_grads.1 = (bf16[4,96,1536]{2,1,0:T(8,128)(2,1)S(1)}, bf16[4,96,1536]{2,1,0:T(8,128)(2,1)S(1)}) custom-call(s32[3]{0:T(128)S(1)} %pad_add_fusion.ids, bf16[1536,768]{1,0:T(8,128)(2,1)S(1)} %bitcast.29, bf16[1536,768]{1,0:T(8,128)(2,1)S(1)} %get-tuple-element.104.grad_keys, bf16[1536,768]{1,0:T(8,128)(2,1)S(1)} %get-tuple-element.105.grad_values), custom_call_target="tpu_custom_call" | custom-call | flops 1000 | bytes 1000 | tf_op jit(solution)/shard_map/key_grads/pallas_call | solution.py:186
  180.9 2.1 ffn_grads.1
  189.7 2.5 collective-permute-done.22.refs_1_
  193.5 14.3 %collective-permute-done.23.refs_2_ = bf16[112,1152]{1,0:T(8,128)(2,1)S(1)} collective-permute-done((bf16[112,1152]{1,0:T(8,128)(2,1)S(1)}, bf16[112,1152]{1,0:T(8,128)(2,1)S(1)}, u32[]{:S(2)}, u32[]{:S(2)}) %collective-permute-start.23) | collective-permute-done | bytes 258080 | tf_op jit(solution)/shard_map/ppermute | solution.py:860
  207.8 2.1 collective-permute-start.36
  211.0 2.2 collective-permute-start.27
  213.2 3.2 %collective-permute-done.36.refs_3_ = bf16[4,96,384]{2,1,0:T(8,128)(2,1)S(1)} collective-permute-done((bf16[4,96,384]{2,1,0:T(8,128)(2,1)S(1)}, bf16[4,96,384]{2,1,0:T(8,128)(2,1)S(1)}, u32[]{:S(2)}, u32[]{:S(2)}) %collective-permute-start.36) | collective-permute-done | bytes 294944 | tf_op jit(solution)/shard_map/ppermute | solution.py:855
  217.5 3.2 %collective-permute-start.38 = (bf16[96,1920]{1,0:T(8,128)(2,1)S(1)}, bf16[96,1920]{1,0:T(8,128)(2,1)S(1)}, u32[]{:S(2)}, u32[]{:S(2)}) collective-permute-start(bf16[96,1920]{1,0:T(8,128)(2,1)S(1)} %get-tuple-element.140), channel_id=1, source_target_pairs={{0,2},{1,3},{2,0},{3,1},{4,6},{5,7},{6,4},{7,5},{8,10},{9,11},{10,... | collective-permute-start | bytes 1105928 | tf_op jit(solution)/shard_map/ppermute | solution.py:860
  222.0 3.8 %collective-permute-start.28 = (bf16[96,1152]{1,0:T(8,128)(2,1)S(1)}, bf16[96,1152]{1,0:T(8,128)(2,1)S(1)}, u32[]{:S(2)}, u32[]{:S(2)}) collective-permute-start(bf16[96,1152]{1,0:T(8,128)(2,1)S(1)} %get-tuple-element.124.refs_0_), channel_id=1, source_target_pairs={{0,4},{4,0},{8,12},{12,8},{16,20},{20,16},{24,28},{28,24},{1,5},{5... | collective-permute-start | bytes 663560 | tf_op jit(solution)/shard_map/ppermute | solution.py:855
  228.3 15.3 %collective-permute-done.38.refs_2_ = bf16[96,1920]{1,0:T(8,128)(2,1)S(1)} collective-permute-done((bf16[96,1920]{1,0:T(8,128)(2,1)S(1)}, bf16[96,1920]{1,0:T(8,128)(2,1)S(1)}, u32[]{:S(2)}, u32[]{:S(2)}) %collective-permute-start.38) | collective-permute-done | bytes 368672 | tf_op jit(solution)/shard_map/ppermute | solution.py:860
  243.5 6.5 %collective-permute-start.31 = (bf16[96,1152]{1,0:T(8,128)(2,1)S(1)}, bf16[96,1152]{1,0:T(8,128)(2,1)S(1)}, u32[]{:S(2)}, u32[]{:S(2)}) collective-permute-start(bf16[96,1152]{1,0:T(8,128)(2,1)S(1)} %collective-permute-done.27.refs_3_), channel_id=1, source_target_pairs={{0,4},{4,0},{8,12},{12,8},{16,20},{20,16},{24,28},{28,24},{1,5},{5... | collective-permute-start | bytes 663560 | tf_op jit(solution)/shard_map/ppermute | solution.py:855
  250.0 3.3 %collective-permute-done.39.refs_3_ = bf16[96,1920]{1,0:T(8,128)(2,1)S(1)} collective-permute-done((bf16[96,1920]{1,0:T(8,128)(2,1)S(1)}, bf16[96,1920]{1,0:T(8,128)(2,1)S(1)}, u32[]{:S(2)}, u32[]{:S(2)}) %collective-permute-start.39) | collective-permute-done | bytes 368672 | tf_op jit(solution)/shard_map/ppermute | solution.py:860
  253.6 2.2 collective-permute-start.42
  256.3 2.1 fusion.1
  259.8 4.4 %collective-permute-done.42.refs_3_ = bf16[96,1920]{1,0:T(8,128)(2,1)S(1)} collective-permute-done((bf16[96,1920]{1,0:T(8,128)(2,1)S(1)}, bf16[96,1920]{1,0:T(8,128)(2,1)S(1)}, u32[]{:S(2)}, u32[]{:S(2)}) %collective-permute-start.42) | collective-permute-done | bytes 368672 | tf_op jit(solution)/shard_map/ppermute | solution.py:855
  264.2 2.3 collective-permute-start.46
  266.5 6.4 %collective-permute-done.41.refs_2_ = bf16[96,1920]{1,0:T(8,128)(2,1)S(1)} collective-permute-done((bf16[96,1920]{1,0:T(8,128)(2,1)S(1)}, bf16[96,1920]{1,0:T(8,128)(2,1)S(1)}, u32[]{:S(2)}, u32[]{:S(2)}) %collective-permute-start.41) | collective-permute-done | bytes 368672 | tf_op jit(solution)/shard_map/ppermute | solution.py:855
  273.5 3.6 %add_convert_fusion = bf16[1536,768]{1,0:T(8,128)(2,1)} fusion(f32[1536,768]{1,0:T(8,128)S(1)} %fusion.1, bf16[1536,768]{1,0:T(8,128)(2,1)S(1)} %get-tuple-element.104.grad_keys, bf16[768,768]{1,0:T(8,128)(2,1)S(1)} %copy-done.32), kind=kOutput, calls=%fused_computation | convolution fusion | flops 1814298624 | bytes 10616832 | tf_op jit(solution)/shard_map/dot_general | solution.py:22
  278.6 2.5 last_out.1
  281.2 3.5 %first_out.1 = (f32[192,3072]{1,0:T(8,128)}, f32[768,768]{1,0:T(8,128)}, f32[192,768]{1,0:T(8,128)}, f32[192,768]{1,0:T(8,128)}) custom-call(s32[3]{0:T(128)S(1)} %pad_add_fusion.ids, bf16[96,1920]{1,0:T(8,128)(2,1)S(1)} %ring_sum.1.refs_0_, bf16[96,1920]{1,0:T(8,128)(2,1)S(1)} %collective-permute-done.40.refs_1_, ...), custom_call_target="tpu_custom_call" | custom-call | flops 1000 | bytes 1000 | tf_op jit(solution)/shard_map/first_out/pallas_call | solution.py:186
  (146 shorter events, 48.8 us)
Async XLA Ops:
  16.3 8.9 %collective-permute-start.2 = (bf16[128,768]{1,0:T(8,128)(2,1)S(1)}, bf16[128,768]{1,0:T(8,128)(2,1)S(1)}, u32[]{:S(2)}, u32[]{:S(2)}) collective-permute-start(bf16[128,768]{1,0:T(8,128)(2,1)S(1)} %get-tuple-element.84.refs_0_), channel_id=1, source_target_pairs={{0,3},{1,0},{2,1},{3,2},{4,7},{5,4},{6,5},{7,6},{8,11},{9,8},{10,9... | collective-permute-start | bytes 589832 | tf_op jit(solution)/shard_map/ppermute | solution.py:860
  16.4 14.8 %collective-permute-start.1 = (bf16[128,768]{1,0:T(8,128)(2,1)S(1)}, bf16[128,768]{1,0:T(8,128)(2,1)S(1)}, u32[]{:S(2)}, u32[]{:S(2)}) collective-permute-start(bf16[128,768]{1,0:T(8,128)(2,1)S(1)} %get-tuple-element.84.refs_0_), channel_id=1, source_target_pairs={{0,2},{1,3},{2,0},{3,1},{4,6},{5,7},{6,4},{7,5},{8,10},{9,11},{10,... | collective-permute-start | bytes 589832 | tf_op jit(solution)/shard_map/ppermute | solution.py:860
  18.9 16.5 %collective-permute-start = (bf16[128,768]{1,0:T(8,128)(2,1)S(1)}, bf16[128,768]{1,0:T(8,128)(2,1)S(1)}, u32[]{:S(2)}, u32[]{:S(2)}) collective-permute-start(bf16[128,768]{1,0:T(8,128)(2,1)S(1)} %get-tuple-element.84.refs_0_), channel_id=1, source_target_pairs={{0,1},{1,2},{2,3},{3,0},{4,5},{5,6},{6,7},{7,4},{8,9},{9,10},{10,1... | collective-permute-start | bytes 589832 | tf_op jit(solution)/shard_map/ppermute | solution.py:860
  42.2 6.9 %collective-permute-start.3 = (bf16[128,896]{1,0:T(8,128)(2,1)S(1)}, bf16[128,896]{1,0:T(8,128)(2,1)S(1)}, u32[]{:S(2)}, u32[]{:S(2)}) collective-permute-start(bf16[128,896]{1,0:T(8,128)(2,1)S(1)} %get-tuple-element.86), channel_id=1, source_target_pairs={{0,3},{1,0},{2,1},{3,2},{4,7},{5,4},{6,5},{7,6},{8,11},{9,8},{10,9... | collective-permute-start | bytes 688136 | tf_op jit(solution)/shard_map/ppermute | solution.py:860
  43.1 14.9 %collective-permute-start.4 = (bf16[128,896]{1,0:T(8,128)(2,1)S(1)}, bf16[128,896]{1,0:T(8,128)(2,1)S(1)}, u32[]{:S(2)}, u32[]{:S(2)}) collective-permute-start(bf16[128,896]{1,0:T(8,128)(2,1)S(1)} %get-tuple-element.87), channel_id=1, source_target_pairs={{0,2},{1,3},{2,0},{3,1},{4,6},{5,7},{6,4},{7,5},{8,10},{9,11},{10,... | collective-permute-start | bytes 688136 | tf_op jit(solution)/shard_map/ppermute | solution.py:860
  45.7 17.2 %collective-permute-start.5 = (bf16[128,896]{1,0:T(8,128)(2,1)S(1)}, bf16[128,896]{1,0:T(8,128)(2,1)S(1)}, u32[]{:S(2)}, u32[]{:S(2)}) collective-permute-start(bf16[128,896]{1,0:T(8,128)(2,1)S(1)} %get-tuple-element.88), channel_id=1, source_target_pairs={{0,1},{1,2},{2,3},{3,0},{4,5},{5,6},{6,7},{7,4},{8,9},{9,10},{10,1... | collective-permute-start | bytes 688136 | tf_op jit(solution)/shard_map/ppermute | solution.py:860
  75.7 7.7 %collective-permute-start.8 = (bf16[128,896]{1,0:T(8,128)(2,1)S(1)}, bf16[128,896]{1,0:T(8,128)(2,1)S(1)}, u32[]{:S(2)}, u32[]{:S(2)}) collective-permute-start(bf16[128,896]{1,0:T(8,128)(2,1)S(1)} %get-tuple-element.98.refs_4_), channel_id=1, source_target_pairs={{0,3},{1,0},{2,1},{3,2},{4,7},{5,4},{6,5},{7,6},{8,11},{9,8},{10,9... | collective-permute-start | bytes 688136 | tf_op jit(solution)/shard_map/ppermute | solution.py:860
  77.9 14.9 %collective-permute-start.7 = (bf16[128,896]{1,0:T(8,128)(2,1)S(1)}, bf16[128,896]{1,0:T(8,128)(2,1)S(1)}, u32[]{:S(2)}, u32[]{:S(2)}) collective-permute-start(bf16[128,896]{1,0:T(8,128)(2,1)S(1)} %get-tuple-element.98.refs_4_), channel_id=1, source_target_pairs={{0,2},{1,3},{2,0},{3,1},{4,6},{5,7},{6,4},{7,5},{8,10},{9,11},{10,... | collective-permute-start | bytes 688136 | tf_op jit(solution)/shard_map/ppermute | solution.py:860
  79.1 18.6 %collective-permute-start.6 = (bf16[128,896]{1,0:T(8,128)(2,1)S(1)}, bf16[128,896]{1,0:T(8,128)(2,1)S(1)}, u32[]{:S(2)}, u32[]{:S(2)}) collective-permute-start(bf16[128,896]{1,0:T(8,128)(2,1)S(1)} %get-tuple-element.98.refs_4_), channel_id=1, source_target_pairs={{0,1},{1,2},{2,3},{3,0},{4,5},{5,6},{6,7},{7,4},{8,9},{9,10},{10,1... | collective-permute-start | bytes 688136 | tf_op jit(solution)/shard_map/ppermute | solution.py:860
  79.1 31.8 %collective-permute-start.12 = (bf16[128,1536]{1,0:T(8,128)(2,1)S(1)}, bf16[128,1536]{1,0:T(8,128)(2,1)S(1)}, u32[]{:S(2)}, u32[]{:S(2)}) collective-permute-start(bf16[128,1536]{1,0:T(8,128)(2,1)S(1)} %get-tuple-element.107), channel_id=1, source_target_pairs={{0,8},{4,12},{8,0},{12,4},{16,24},{20,28},{24,16},{28,20},{1,9},{5... | collective-permute-start | bytes 1179656 | tf_op jit(solution)/shard_map/ppermute | solution.py:855
  80.3 48.1 %copy-start.10 = (bf16[768,768]{1,0:T(8,128)(2,1)S(1)}, bf16[768,768]{1,0:T(8,128)(2,1)}, u32[]{:S(2)}) copy-start(bf16[768,768]{1,0:T(8,128)(2,1)} %refs_0_.3) | copy-start | bytes 3538948
  80.4 59.8 %collective-permute-start.13 = (bf16[128,1536]{1,0:T(8,128)(2,1)}, bf16[128,1536]{1,0:T(8,128)(2,1)S(1)}, u32[]{:S(2)}, u32[]{:S(2)}) collective-permute-start(bf16[128,1536]{1,0:T(8,128)(2,1)} %get-tuple-element.108), channel_id=1, source_target_pairs={{0,16},{4,20},{8,24},{12,28},{16,0},{20,4},{24,8},{28,12},{1,17},{... | collective-permute-start | bytes 1179656 | tf_op jit(solution)/shard_map/ppermute | solution.py:855
  107.5 7.1 %collective-permute-start.9 = (bf16[128,768]{1,0:T(8,128)(2,1)S(1)}, bf16[128,768]{1,0:T(8,128)(2,1)S(1)}, u32[]{:S(2)}, u32[]{:S(2)}) collective-permute-start(bf16[128,768]{1,0:T(8,128)(2,1)S(1)} %get-tuple-element.100), channel_id=1, source_target_pairs={{0,3},{1,0},{2,1},{3,2},{4,7},{5,4},{6,5},{7,6},{8,11},{9,8},{10,9... | collective-permute-start | bytes 589832 | tf_op jit(solution)/shard_map/ppermute | solution.py:860
  109.2 12.8 %collective-permute-start.10 = (bf16[128,768]{1,0:T(8,128)(2,1)S(1)}, bf16[128,768]{1,0:T(8,128)(2,1)S(1)}, u32[]{:S(2)}, u32[]{:S(2)}) collective-permute-start(bf16[128,768]{1,0:T(8,128)(2,1)S(1)} %get-tuple-element.101), channel_id=1, source_target_pairs={{0,2},{1,3},{2,0},{3,1},{4,6},{5,7},{6,4},{7,5},{8,10},{9,11},{10,... | collective-permute-start | bytes 589832 | tf_op jit(solution)/shard_map/ppermute | solution.py:860
  110.9 15.3 %collective-permute-start.11 = (bf16[128,768]{1,0:T(8,128)(2,1)S(1)}, bf16[128,768]{1,0:T(8,128)(2,1)S(1)}, u32[]{:S(2)}, u32[]{:S(2)}) collective-permute-start(bf16[128,768]{1,0:T(8,128)(2,1)S(1)} %get-tuple-element.102), channel_id=1, source_target_pairs={{0,1},{1,2},{2,3},{3,0},{4,5},{5,6},{6,7},{7,4},{8,9},{9,10},{10,1... | collective-permute-start | bytes 589832 | tf_op jit(solution)/shard_map/ppermute | solution.py:860
  110.9 58.7 %collective-permute-start.15 = (bf16[128,3072]{1,0:T(8,128)(2,1)}, bf16[128,3072]{1,0:T(8,128)(2,1)S(1)}, u32[]{:S(2)}, u32[]{:S(2)}) collective-permute-start(bf16[128,3072]{1,0:T(8,128)(2,1)} %get-tuple-element.111), channel_id=1, source_target_pairs={{0,8},{4,12},{8,0},{12,4},{16,24},{20,28},{24,16},{28,20},{1,9},{5... | collective-permute-start | bytes 2359304 | tf_op jit(solution)/shard_map/ppermute | solution.py:855
  114.6 55.1 %collective-permute-start.16 = (bf16[128,3072]{1,0:T(8,128)(2,1)}, bf16[128,3072]{1,0:T(8,128)(2,1)S(1)}, u32[]{:S(2)}, u32[]{:S(2)}) collective-permute-start(bf16[128,3072]{1,0:T(8,128)(2,1)} %get-tuple-element.112), channel_id=1, source_target_pairs={{0,16},{4,20},{8,24},{12,28},{16,0},{20,4},{24,8},{28,12},{1,17},{... | collective-permute-start | bytes 2359304 | tf_op jit(solution)/shard_map/ppermute | solution.py:855
  122.0 47.7 %collective-permute-start.17 = (bf16[128,3072]{1,0:T(8,128)(2,1)}, bf16[128,3072]{1,0:T(8,128)(2,1)S(1)}, u32[]{:S(2)}, u32[]{:S(2)}) collective-permute-start(bf16[128,3072]{1,0:T(8,128)(2,1)} %copy-done.28), channel_id=1, source_target_pairs={{0,24},{4,28},{8,16},{12,20},{16,8},{20,12},{24,0},{28,4},{1,25},{... | collective-permute-start | bytes 2359304 | tf_op jit(solution)/shard_map/ppermute | solution.py:855
  126.2 29.1 %collective-permute-start.14 = (bf16[128,1536]{1,0:T(8,128)(2,1)}, bf16[128,1536]{1,0:T(8,128)(2,1)S(1)}, u32[]{:S(2)}, u32[]{:S(2)}) collective-permute-start(bf16[128,1536]{1,0:T(8,128)(2,1)} %copy-done.29), channel_id=1, source_target_pairs={{0,24},{4,28},{8,16},{12,20},{16,8},{20,12},{24,0},{28,4},{1,25},{... | collective-permute-start | bytes 1179656 | tf_op jit(solution)/shard_map/ppermute | solution.py:855
  140.2 21.2 %collective-permute-start.18 = (bf16[144,1152]{1,0:T(8,128)(2,1)S(1)}, bf16[144,1152]{1,0:T(8,128)(2,1)S(1)}, u32[]{:S(2)}, u32[]{:S(2)}) collective-permute-start(bf16[144,1152]{1,0:T(8,128)(2,1)S(1)} %get-tuple-element.115), channel_id=1, source_target_pairs={{0,8},{4,12},{8,0},{12,4},{16,24},{20,28},{24,16},{28,20},{1,9},{5... | collective-permute-start | bytes 995336 | tf_op jit(solution)/shard_map/ppermute | solution.py:855
  155.3 8.8 %collective-permute-start.19 = (bf16[144,1152]{1,0:T(8,128)(2,1)S(1)}, bf16[144,1152]{1,0:T(8,128)(2,1)S(1)}, u32[]{:S(2)}, u32[]{:S(2)}) collective-permute-start(bf16[144,1152]{1,0:T(8,128)(2,1)S(1)} %get-tuple-element.116), channel_id=1, source_target_pairs={{0,16},{4,20},{8,24},{12,28},{16,0},{20,4},{24,8},{28,12},{1,17},{... | collective-permute-start | bytes 995336 | tf_op jit(solution)/shard_map/ppermute | solution.py:855
  161.5 8.2 %collective-permute-start.20 = (bf16[144,1152]{1,0:T(8,128)(2,1)S(1)}, bf16[144,1152]{1,0:T(8,128)(2,1)S(1)}, u32[]{:S(2)}, u32[]{:S(2)}) collective-permute-start(bf16[144,1152]{1,0:T(8,128)(2,1)S(1)} %get-tuple-element.117), channel_id=1, source_target_pairs={{0,24},{4,28},{8,16},{12,20},{16,8},{20,12},{24,0},{28,4},{1,25},{... | collective-permute-start | bytes 995336 | tf_op jit(solution)/shard_map/ppermute | solution.py:855
  171.6 12.0 %collective-permute-start.21 = (bf16[4,112,1152]{2,1,0:T(8,128)(2,1)S(1)}, bf16[4,112,1152]{2,1,0:T(8,128)(2,1)S(1)}, u32[]{:S(2)}, u32[]{:S(2)}) collective-permute-start(bf16[4,112,1152]{2,1,0:T(8,128)(2,1)S(1)} %get-tuple-element.119), channel_id=1, source_target_pairs={{0,4},{4,0},{8,12},{12,8},{16,20},{20,16},{24,28},{28,24},{1,5},{5... | collective-permute-start | bytes 3096584 | tf_op jit(solution)/shard_map/ppermute | solution.py:855
  180.8 6.4 %collective-permute-start.33 = (bf16[4,96,1536]{2,1,0:T(8,128)(2,1)S(1)}, bf16[4,96,1536]{2,1,0:T(8,128)(2,1)S(1)}, u32[]{:S(2)}, u32[]{:S(2)}) collective-permute-start(bf16[4,96,1536]{2,1,0:T(8,128)(2,1)S(1)} %get-tuple-element.133), channel_id=1, source_target_pairs={{0,4},{4,0},{8,12},{12,8},{16,20},{20,16},{24,28},{28,24},{1,5},{5... | collective-permute-start | bytes 3538952 | tf_op jit(solution)/shard_map/ppermute | solution.py:855
  183.1 33.4 %collective-permute-start.32 = (bf16[4,96,1536]{2,1,0:T(8,128)(2,1)S(1)}, bf16[4,96,1536]{2,1,0:T(8,128)(2,1)S(1)}, u32[]{:S(2)}, u32[]{:S(2)}) collective-permute-start(bf16[4,96,1536]{2,1,0:T(8,128)(2,1)S(1)} %get-tuple-element.131), channel_id=1, source_target_pairs={{0,4},{4,0},{8,12},{12,8},{16,20},{20,16},{24,28},{28,24},{1,5},{5... | collective-permute-start | bytes 3538952 | tf_op jit(solution)/shard_map/ppermute | solution.py:855
  184.4 7.9 %collective-permute-start.22 = (bf16[112,1152]{1,0:T(8,128)(2,1)S(1)}, bf16[112,1152]{1,0:T(8,128)(2,1)S(1)}, u32[]{:S(2)}, u32[]{:S(2)}) collective-permute-start(bf16[112,1152]{1,0:T(8,128)(2,1)S(1)} %get-tuple-element.121), channel_id=1, source_target_pairs={{0,1},{1,2},{2,3},{3,0},{4,5},{5,6},{6,7},{7,4},{8,9},{9,10},{10,1... | collective-permute-start | bytes 774152 | tf_op jit(solution)/shard_map/ppermute | solution.py:860
  185.6 22.2 %collective-permute-start.23 = (bf16[112,1152]{1,0:T(8,128)(2,1)S(1)}, bf16[112,1152]{1,0:T(8,128)(2,1)S(1)}, u32[]{:S(2)}, u32[]{:S(2)}) collective-permute-start(bf16[112,1152]{1,0:T(8,128)(2,1)S(1)} %get-tuple-element.122), channel_id=1, source_target_pairs={{0,2},{1,3},{2,0},{3,1},{4,6},{5,7},{6,4},{7,5},{8,10},{9,11},{10,... | collective-permute-start | bytes 774152 | tf_op jit(solution)/shard_map/ppermute | solution.py:860
  187.2 23.1 %collective-permute-start.24 = (bf16[112,1152]{1,0:T(8,128)(2,1)S(1)}, bf16[112,1152]{1,0:T(8,128)(2,1)S(1)}, u32[]{:S(2)}, u32[]{:S(2)}) collective-permute-start(bf16[112,1152]{1,0:T(8,128)(2,1)S(1)} %get-tuple-element.123), channel_id=1, source_target_pairs={{0,3},{1,0},{2,1},{3,2},{4,7},{5,4},{6,5},{7,6},{8,11},{9,8},{10,9... | collective-permute-start | bytes 774152 | tf_op jit(solution)/shard_map/ppermute | solution.py:860
  188.5 24.7 %collective-permute-start.34 = (bf16[4,96,384]{2,1,0:T(8,128)(2,1)S(1)}, bf16[4,96,384]{2,1,0:T(8,128)(2,1)S(1)}, u32[]{:S(2)}, u32[]{:S(2)}) collective-permute-start(bf16[4,96,384]{2,1,0:T(8,128)(2,1)S(1)} %get-tuple-element.135), channel_id=1, source_target_pairs={{0,8},{4,12},{8,0},{12,4},{16,24},{20,28},{24,16},{28,20},{1,9},{5... | collective-permute-start | bytes 884744 | tf_op jit(solution)/shard_map/ppermute | solution.py:855
  192.3 20.9 %collective-permute-start.35 = (bf16[4,96,384]{2,1,0:T(8,128)(2,1)S(1)}, bf16[4,96,384]{2,1,0:T(8,128)(2,1)S(1)}, u32[]{:S(2)}, u32[]{:S(2)}) collective-permute-start(bf16[4,96,384]{2,1,0:T(8,128)(2,1)S(1)} %get-tuple-element.136), channel_id=1, source_target_pairs={{0,16},{4,20},{8,24},{12,28},{16,0},{20,4},{24,8},{28,12},{1,17},{... | collective-permute-start | bytes 884744 | tf_op jit(solution)/shard_map/ppermute | solution.py:855
  207.8 8.6 %collective-permute-start.36 = (bf16[4,96,384]{2,1,0:T(8,128)(2,1)S(1)}, bf16[4,96,384]{2,1,0:T(8,128)(2,1)S(1)}, u32[]{:S(2)}, u32[]{:S(2)}) collective-permute-start(bf16[4,96,384]{2,1,0:T(8,128)(2,1)S(1)} %get-tuple-element.137), channel_id=1, source_target_pairs={{0,24},{4,28},{8,16},{12,20},{16,8},{20,12},{24,0},{28,4},{1,25},{... | collective-permute-start | bytes 884744 | tf_op jit(solution)/shard_map/ppermute | solution.py:855
  211.0 14.8 %collective-permute-start.27 = (bf16[96,1152]{1,0:T(8,128)(2,1)S(1)}, bf16[96,1152]{1,0:T(8,128)(2,1)S(1)}, u32[]{:S(2)}, u32[]{:S(2)}) collective-permute-start(bf16[96,1152]{1,0:T(8,128)(2,1)S(1)} %get-tuple-element.124.refs_0_), channel_id=1, source_target_pairs={{0,24},{4,28},{8,16},{12,20},{16,8},{20,12},{24,0},{28,4},{1,25},{... | collective-permute-start | bytes 663560 | tf_op jit(solution)/shard_map/ppermute | solution.py:855
  217.4 9.7 %collective-permute-start.37 = (bf16[96,1920]{1,0:T(8,128)(2,1)S(1)}, bf16[96,1920]{1,0:T(8,128)(2,1)S(1)}, u32[]{:S(2)}, u32[]{:S(2)}) collective-permute-start(bf16[96,1920]{1,0:T(8,128)(2,1)S(1)} %get-tuple-element.139), channel_id=1, source_target_pairs={{0,1},{1,2},{2,3},{3,0},{4,5},{5,6},{6,7},{7,4},{8,9},{9,10},{10,1... | collective-permute-start | bytes 1105928 | tf_op jit(solution)/shard_map/ppermute | solution.py:860
  217.5 26.1 %collective-permute-start.38 = (bf16[96,1920]{1,0:T(8,128)(2,1)S(1)}, bf16[96,1920]{1,0:T(8,128)(2,1)S(1)}, u32[]{:S(2)}, u32[]{:S(2)}) collective-permute-start(bf16[96,1920]{1,0:T(8,128)(2,1)S(1)} %get-tuple-element.140), channel_id=1, source_target_pairs={{0,2},{1,3},{2,0},{3,1},{4,6},{5,7},{6,4},{7,5},{8,10},{9,11},{10,... | collective-permute-start | bytes 1105928 | tf_op jit(solution)/shard_map/ppermute | solution.py:860
  220.6 32.7 %collective-permute-start.39 = (bf16[96,1920]{1,0:T(8,128)(2,1)S(1)}, bf16[96,1920]{1,0:T(8,128)(2,1)S(1)}, u32[]{:S(2)}, u32[]{:S(2)}) collective-permute-start(bf16[96,1920]{1,0:T(8,128)(2,1)S(1)} %get-tuple-element.141), channel_id=1, source_target_pairs={{0,3},{1,0},{2,1},{3,2},{4,7},{5,4},{6,5},{7,6},{8,11},{9,8},{10,9... | collective-permute-start | bytes 1105928 | tf_op jit(solution)/shard_map/ppermute | solution.py:860
  222.0 33.7 %collective-permute-start.28 = (bf16[96,1152]{1,0:T(8,128)(2,1)S(1)}, bf16[96,1152]{1,0:T(8,128)(2,1)S(1)}, u32[]{:S(2)}, u32[]{:S(2)}) collective-permute-start(bf16[96,1152]{1,0:T(8,128)(2,1)S(1)} %get-tuple-element.124.refs_0_), channel_id=1, source_target_pairs={{0,4},{4,0},{8,12},{12,8},{16,20},{20,16},{24,28},{28,24},{1,5},{5... | collective-permute-start | bytes 663560 | tf_op jit(solution)/shard_map/ppermute | solution.py:855
  225.8 30.2 %collective-permute-start.26 = (bf16[96,1152]{1,0:T(8,128)(2,1)S(1)}, bf16[96,1152]{1,0:T(8,128)(2,1)S(1)}, u32[]{:S(2)}, u32[]{:S(2)}) collective-permute-start(bf16[96,1152]{1,0:T(8,128)(2,1)S(1)} %get-tuple-element.124.refs_0_), channel_id=1, source_target_pairs={{0,16},{4,20},{8,24},{12,28},{16,0},{20,4},{24,8},{28,12},{1,17},{... | collective-permute-start | bytes 663560 | tf_op jit(solution)/shard_map/ppermute | solution.py:855
  227.1 31.3 %collective-permute-start.25 = (bf16[96,1152]{1,0:T(8,128)(2,1)S(1)}, bf16[96,1152]{1,0:T(8,128)(2,1)S(1)}, u32[]{:S(2)}, u32[]{:S(2)}) collective-permute-start(bf16[96,1152]{1,0:T(8,128)(2,1)S(1)} %get-tuple-element.124.refs_0_), channel_id=1, source_target_pairs={{0,8},{4,12},{8,0},{12,4},{16,24},{20,28},{24,16},{28,20},{1,9},{5... | collective-permute-start | bytes 663560 | tf_op jit(solution)/shard_map/ppermute | solution.py:855
  243.5 16.2 %collective-permute-start.31 = (bf16[96,1152]{1,0:T(8,128)(2,1)S(1)}, bf16[96,1152]{1,0:T(8,128)(2,1)S(1)}, u32[]{:S(2)}, u32[]{:S(2)}) collective-permute-start(bf16[96,1152]{1,0:T(8,128)(2,1)S(1)} %collective-permute-done.27.refs_3_), channel_id=1, source_target_pairs={{0,4},{4,0},{8,12},{12,8},{16,20},{20,16},{24,28},{28,24},{1,5},{5... | collective-permute-start | bytes 663560 | tf_op jit(solution)/shard_map/ppermute | solution.py:855
  253.6 10.7 %collective-permute-start.42 = (bf16[96,1920]{1,0:T(8,128)(2,1)S(1)}, bf16[96,1920]{1,0:T(8,128)(2,1)S(1)}, u32[]{:S(2)}, u32[]{:S(2)}) collective-permute-start(bf16[96,1920]{1,0:T(8,128)(2,1)S(1)} %ring_sum.1.refs_0_), channel_id=1, source_target_pairs={{0,24},{4,28},{8,16},{12,20},{16,8},{20,12},{24,0},{28,4},{1,25},{... | collective-permute-start | bytes 1105928 | tf_op jit(solution)/shard_map/ppermute | solution.py:855
  255.7 17.2 %collective-permute-start.41 = (bf16[96,1920]{1,0:T(8,128)(2,1)S(1)}, bf16[96,1920]{1,0:T(8,128)(2,1)S(1)}, u32[]{:S(2)}, u32[]{:S(2)}) collective-permute-start(bf16[96,1920]{1,0:T(8,128)(2,1)S(1)} %ring_sum.1.refs_0_), channel_id=1, source_target_pairs={{0,16},{4,20},{8,24},{12,28},{16,0},{20,4},{24,8},{28,12},{1,17},{... | collective-permute-start | bytes 1105928 | tf_op jit(solution)/shard_map/ppermute | solution.py:855
  256.0 17.4 %collective-permute-start.40 = (bf16[96,1920]{1,0:T(8,128)(2,1)S(1)}, bf16[96,1920]{1,0:T(8,128)(2,1)S(1)}, u32[]{:S(2)}, u32[]{:S(2)}) collective-permute-start(bf16[96,1920]{1,0:T(8,128)(2,1)S(1)} %ring_sum.1.refs_0_), channel_id=1, source_target_pairs={{0,8},{4,12},{8,0},{12,4},{16,24},{20,28},{24,16},{28,20},{1,9},{5... | collective-permute-start | bytes 1105928 | tf_op jit(solution)/shard_map/ppermute | solution.py:855
  258.4 18.7 %collective-permute-start.30 = (bf16[96,1152]{1,0:T(8,128)(2,1)S(1)}, bf16[96,1152]{1,0:T(8,128)(2,1)S(1)}, u32[]{:S(2)}, u32[]{:S(2)}) collective-permute-start(bf16[96,1152]{1,0:T(8,128)(2,1)S(1)} %collective-permute-done.26.refs_2_), channel_id=1, source_target_pairs={{0,4},{4,0},{8,12},{12,8},{16,20},{20,16},{24,28},{28,24},{1,5},{5... | collective-permute-start | bytes 663560 | tf_op jit(solution)/shard_map/ppermute | solution.py:855
  259.8 21.4 %collective-permute-start.43 = (bf16[96,1920]{1,0:T(8,128)(2,1)S(1)}, bf16[96,1920]{1,0:T(8,128)(2,1)S(1)}, u32[]{:S(2)}, u32[]{:S(2)}) collective-permute-start(bf16[96,1920]{1,0:T(8,128)(2,1)S(1)} %ring_sum.1.refs_0_), channel_id=1, source_target_pairs={{0,4},{4,0},{8,12},{12,8},{16,20},{20,16},{24,28},{28,24},{1,5},{5... | collective-permute-start | bytes 1105928 | tf_op jit(solution)/shard_map/ppermute | solution.py:855
  264.2 16.9 %collective-permute-start.46 = (bf16[96,1920]{1,0:T(8,128)(2,1)S(1)}, bf16[96,1920]{1,0:T(8,128)(2,1)S(1)}, u32[]{:S(2)}, u32[]{:S(2)}) collective-permute-start(bf16[96,1920]{1,0:T(8,128)(2,1)S(1)} %collective-permute-done.42.refs_3_), channel_id=1, source_target_pairs={{0,4},{4,0},{8,12},{12,8},{16,20},{20,16},{24,28},{28,24},{1,5},{5... | collective-permute-start | bytes 1105928 | tf_op jit(solution)/shard_map/ppermute | solution.py:855
  272.9 8.2 %collective-permute-start.45 = (bf16[96,1920]{1,0:T(8,128)(2,1)S(1)}, bf16[96,1920]{1,0:T(8,128)(2,1)S(1)}, u32[]{:S(2)}, u32[]{:S(2)}) collective-permute-start(bf16[96,1920]{1,0:T(8,128)(2,1)S(1)} %collective-permute-done.41.refs_2_), channel_id=1, source_target_pairs={{0,4},{4,0},{8,12},{12,8},{16,20},{20,16},{24,28},{28,24},{1,5},{5... | collective-permute-start | bytes 1105928 | tf_op jit(solution)/shard_map/ppermute | solution.py:855
  273.4 7.7 %collective-permute-start.44 = (bf16[96,1920]{1,0:T(8,128)(2,1)S(1)}, bf16[96,1920]{1,0:T(8,128)(2,1)S(1)}, u32[]{:S(2)}, u32[]{:S(2)}) collective-permute-start(bf16[96,1920]{1,0:T(8,128)(2,1)S(1)} %collective-permute-done.40.refs_1_), channel_id=1, source_target_pairs={{0,4},{4,0},{8,12},{12,8},{16,20},{20,16},{24,28},{28,24},{1,5},{5... | collective-permute-start | bytes 1105928 | tf_op jit(solution)/shard_map/ppermute | solution.py:855
  277.1 1.5 collective-permute-start.29
  (36 other events, 630.2 us)
where the time goes:
time: 285 us
  waiting for transfers between devices  131 us (46%)
  starting transfers between devices  66.7 us (23%)
  Pallas kernels  60.1 us (21%)
  local copies, waits for them, and re-layouts  15.7 us (6%)
  matrix products  9.73 us (3%)
    ppermute x18, waiting for transfers between devices, shift(): lax.ppermute(values, axis, [(i, (i + by) % peers) for i in range(peers)])  89.9 us
    ppermute x29, starting transfers between devices, swap(): return lax.ppermute(values, axis, [(i, i ^ by) for i in range(peers)])  44.2 us
    pallas_call x13, Pallas kernels, call(): pl.pallas_call(kernel, out_shape=outs, in_specs=specs, out_specs=jax.tree...  43.5 us
    ppermute x29, waiting for transfers between devices, swap(): return lax.ppermute(values, axis, [(i, i ^ by) for i in range(peers)])  41.3 us
    ppermute x18, starting transfers between devices, shift(): lax.ppermute(values, axis, [(i, (i + by) % peers) for i in range(peers)])  22.4 us
    unnamed x74, local copies, waits for them, and re-layouts  13.7 us
    pallas_call x1, Pallas kernels, cross_backward(): pl.pallas_call(cross_backward_kernel, grid_spec=pltpu.PrefetchScalarGridS...  9.8 us
    dot_general x4, matrix products, dot(): lax.dot_general(left, right, (((left_dim,), (right_dim,)), ((), ())), pre...  9.73 us
  transfers between devices with their start and end apart: 47, of which 24 were waited for; matrix products, arithmetic and copies ran while one was open for 4% of the time, Pallas kernels for 11%

commit v1 on v0

v1 whole, which is shorter than its diff:
```python
import functools

import jax
import jax.numpy as jnp
from jax import lax
from jax.experimental import pallas as pl
from jax.experimental.pallas import tpu as pltpu
from jax.sharding import PartitionSpec as P

HEADS = 12
EPS = 1e-06
NEG = -1000000000.0
F32 = jnp.float32
BF = jnp.bfloat16
SLOTS = 8
LANES = 128
MIB = 1 << 20


def dot(left, right, left_dim, right_dim, precision=None):
    return lax.dot_general(
        left,
        right,
        (((left_dim,), (right_dim,)), ((), ())),
        precision=precision,
        preferred_element_type=F32,
    )


def nn(left, right):
    return dot(left, right, 1, 0)


def nt(left, right):
    return dot(left, right, 1, 1)


def tn(left, right):
    return dot(left, right, 0, 0)


def low(values):
    return values.astype(BF)


def inverse_rms(values):
    return lax.rsqrt(jnp.mean(values * values, axis=-1, keepdims=True) + EPS)


def norm_back(grad, values, gain):
    inv = inverse_rms(values)
    scaled = gain * grad
    inner = jnp.mean(values * scaled, axis=-1, keepdims=True)
    grad_values = inv * scaled - values * (inv * inv * inv * inner)
    grad_gain = jnp.sum(grad * values * inv, axis=0, keepdims=True)
    return grad_values, grad_gain


def lanes_of(shape):
    return lax.broadcasted_iota(jnp.int32, shape, len(shape) - 1)


def rows_of(shape):
    return lax.broadcasted_iota(jnp.int32, shape, len(shape) - 2)


def ones_where(condition):
    return jnp.where(condition, 1.0, 0.0).astype(BF)


def spread_matrix(width):
    slot, lane = rows_of((LANES, width)), lanes_of((LANES, width))
    return ones_where((slot // SLOTS == lane // (width // HEADS)) & (slot % SLOTS < 3))


def compact_matrix():
    slot, lane = rows_of((LANES, LANES)), lanes_of((LANES, LANES))
    return ones_where((slot // SLOTS == lane // SLOTS) & (slot % SLOTS < 3))


def gather_matrix(width):
    feature, lane = rows_of((width, LANES)), lanes_of((width, LANES))
    return ones_where(feature // (width // HEADS) == lane // SLOTS)


def split_three(values):
    first = low(values).astype(F32)
    rest = values - first
    second = low(rest).astype(F32)
    third = low(rest - second).astype(F32)
    return first, second, third


def in_slots(values, start=0):
    first, second, third = split_three(values)
    slot = lanes_of(values.shape) % SLOTS - start
    return jnp.where(slot == 0, first, jnp.where(slot == 1, second, jnp.where(slot == 2, third, 0.0)))


def head_sums(values, matrix):
    first, second, third = split_three(values)
    return nn(low(first), matrix) + nn(low(second), matrix) + nn(low(third), matrix)


def two_heads(block):
    first = lanes_of(block.shape) < block.shape[1] // 2
    zero = jnp.zeros_like(block)
    return jnp.concatenate([jnp.where(first, block, zero), jnp.where(first, zero, block)], 0)


def fold_heads(block):
    half = block.shape[0] // 2
    lane = lanes_of((half, block.shape[1]))
    return jnp.where(lane < block.shape[1] // 2, block[:half], block[half:])


def pair_of_slots(extra, pair, start, more=None):
    lane = lanes_of(extra.shape)
    slot = lane % SLOTS
    wanted = (slot >= start) & (slot < start + 3)
    halves = [
        jnp.where(wanted & (lane // SLOTS == 2 * pair + i), extra, jnp.zeros_like(extra)) for i in range(2)
    ]
    block = jnp.concatenate(halves, 0)
    return block if more is None else block + more


def last_lane(rows, value):
    return jnp.where(lanes_of((rows, LANES)) == LANES - 1, value, 0.0).astype(BF)


def attend_pair(queries, keys, values, valid=None):
    scores = nt(keys, queries)
    if valid is not None:
        scores = jnp.where(valid, scores, NEG)
    top = jnp.max(scores, axis=0, keepdims=True)
    weights = low(jnp.exp(scores - top))
    both = tn(weights, values)
    split = both.shape[1] - LANES
    mixture = fold_heads(both[:, :split]) * (1.0 / fold_heads(both[:, split:]))
    return mixture, both[:, split:], top


def log_totals(sums, tops):
    tokens = tops[0].shape[1] // 2
    lane = lanes_of((tokens, LANES)) // SLOTS
    found = jnp.ones((tokens, LANES), F32)
    rows = []
    for pair, (both, top) in enumerate(zip(sums, tops)):
        found = jnp.where(lane == 2 * pair, both[:tokens], jnp.where(lane == 2 * pair + 1, both[tokens:], found))
        rows += [jnp.broadcast_to(top[:, :tokens], (SLOTS, tokens)), jnp.broadcast_to(top[:, tokens:], (SLOTS, tokens))]
    rows.append(jnp.zeros((LANES - HEADS * SLOTS, tokens), F32))
    return jnp.transpose(jnp.concatenate(rows, 0)) + jnp.log(found)


def attend_pair_back(queries, keys, values, grad_mix, query_more, key_more, grad_more, value_more, valid=None):
    scaled = two_heads(queries)
    grad_two = two_heads(grad_mix)
    scores = nt(jnp.concatenate([keys, key_more], 1), jnp.concatenate([scaled, query_more], 1))
    probs = jnp.exp(scores)
    if valid is not None:
        probs = jnp.where(valid, probs, 0.0)
    grad_probs = nt(jnp.concatenate([values, value_more], 1), jnp.concatenate([grad_two, grad_more], 1))
    grad_scores = low(probs * grad_probs)
    grad_values = nn(low(probs), grad_two)
    grad_keys = nn(grad_scores, scaled)
    grad_queries = fold_heads(tn(grad_scores, keys))
    return grad_queries, grad_keys, grad_values


def minus_slots(rows, start):
    slot = lanes_of((rows, LANES)) % SLOTS
    return jnp.where((slot >= start) & (slot < start + 3), -1.0, 0.0)


def causal_mask(tokens):
    key = rows_of((tokens, 2 * tokens))
    token = lanes_of((tokens, 2 * tokens))
    return key <= jnp.where(token >= tokens, token - tokens, token)


WEIGHTS = {
    "self_forward": 0,
    "key_values": 5,
    "cross_forward": 1,
    "feed_forward": 5,
    "cross_backward": 0,
    "key_grads": 6,
    "ffn_grads": 0,
    "first_sum": 0,
    "self_backward": 20,
    "encoder_grad": 0,
    "ring_sum": 0,
    "tail_grads": 0,
    "tail_sum": 0,
    "first_out": 0,
    "last_sum": 0,
    "last_out": 0,
    "meet": 0,
    "pack": 0,
    "hold": 0,
    "key_sum": 0,
    "key_add": 0,
    "first_add": 0,
}


class Line:
    def __init__(self):
        self.token = None

    def __call__(self, kernel, name, outs, args, mib, scratch=(), places="", after=(), weight=None):
        kinds = {"s": pltpu.SMEM, "h": pltpu.HBM, "v": pltpu.VMEM}
        placed = places[:1] == "i"
        specs = [pl.BlockSpec(memory_space=kinds[letter]) for letter in places[placed:]]
        count = len(args)
        single = not isinstance(outs, (tuple, list))
        outs = ((outs,) if single else tuple(outs)) + (shape32(SLOTS, LANES),)
        given = (() if self.token is None else (self.token,)) + tuple(after)
        homes = [pltpu.HBM if name == "self_forward" else pltpu.VMEM] * (len(outs) - 1) + [pltpu.VMEM]

        def run(*refs):
            at = count + len(given)
            made = refs[at : at + len(outs)]
            made[-1][...] = jnp.zeros((SLOTS, LANES), F32)
            here = ()
            if placed:
                lane = lax.axis_index("pb").astype(jnp.int32)
                here = ((lax.axis_index("pa").astype(jnp.int32), lane >> 1, lane & 1),)
            kernel(*here, *refs[:count], *made[:-1], *refs[at + len(outs) :])

        found = pl.pallas_call(
            run,
            out_shape=outs,
            in_specs=specs + [pl.BlockSpec(memory_space=pl.ANY)] * len(given),
            out_specs=[pl.BlockSpec(memory_space=home) for home in homes],
            scratch_shapes=scratch,
            compiler_params=pltpu.CompilerParams(vmem_limit_bytes=mib * MIB),
            cost_estimate=pl.CostEstimate(flops=int(1153000000 * (WEIGHTS[name] if weight is None else weight)), bytes_accessed=0, transcendentals=0),
            name=name,
        )(*args, *given)
        self.token = found[-1]
        return found[0] if single else found[:-1]

    def meet(self, weight, after=()):
        self(lambda *refs: None, "meet", (), (), 4, (), "", after, weight)


def shape(*dims):
    return jax.ShapeDtypeStruct(dims, BF)


def shape32(*dims):
    return jax.ShapeDtypeStruct(dims, F32)


def row(gain):
    return gain[...].reshape(1, gain.shape[0])


def self_forward_kernel(ids, *refs, chips):
    far, refs = refs[:9], refs[9:]
    outs, early = refs[:8], refs[8 : 8 + chips]
    held, made, mix_held, (sems, out_sems, early_sems) = (
        refs[8 + chips : 17 + chips], refs[17 + chips : 25 + chips], refs[25 + chips], refs[26 + chips :]
    )
    copies = [pltpu.make_async_copy(item, near, sems.at[i]) for i, (item, near) in enumerate(zip(far, held))]
    for item in copies:
        item.start()
    hidden, cot, gain_self, gain_cross = held[:4]
    weights = held[4:]
    q_out, k_out, v_out, mixture_out, logs_out, after_out, x_cross_out, cross_q_out = made
    x_held = mix_held.at[0]
    mixes = mix_held.at[1]
    pending = []

    def send(index):
        pending.append(pltpu.make_async_copy(made[index], outs[index], out_sems.at[index]))
        pending[-1].start()

    width = hidden.shape[1]
    tokens = hidden.shape[0]
    factor = (width // HEADS) ** -0.5
    copies[0].wait()
    copies[2].wait()
    stream = hidden[...].astype(F32)
    x_self = low(stream * inverse_rms(stream) * row(gain_self))
    x_held[...] = x_self
    for i in range(3):
        copies[4 + i].wait()
        made[i][...] = low(nn(x_self, weights[i][...]))
        send(i)
    queries, keys, values = (made[i][...] for i in range(3))
    copies[1].wait()
    for by, out in enumerate(early):
        pending.append(pltpu.make_async_copy(cot, out.at[:, pl.ds(width, width)], early_sems.at[2 * by]))
        pending[-1].start()
    valid = causal_mask(tokens)
    pair_width = 2 * width // HEADS
    ones = jnp.ones((tokens, LANES), BF)
    mixtures, sums, tops = [], [], []
    for pair in range(HEADS // 2):
        part = slice(pair * pair_width, (pair + 1) * pair_width)
        mixture, both, top = attend_pair(
            two_heads(queries[:, part] * factor), keys[:, part], jnp.concatenate([values[:, part], ones], 1), valid
        )
        mixtures.append(mixture)
        sums.append(both)
        tops.append(top)
    mixture = jnp.concatenate(mixtures, 1)
    mixture_out[...] = mixture
    send(3)
    logs_out[...] = log_totals(sums, tops)
    send(4)
    mix = low(mixture)
    mixes[...] = mix
    chip = ids[1]
    for by, out in enumerate(early):
        last = lax.div((chip ^ by) * 4, chips) == 3
        place = out.at[:, pl.ds(0, width)]

        @pl.when(last)
        def _():
            pltpu.make_async_copy(mixes, place, early_sems.at[2 * by + 1]).start()

        @pl.when(jnp.logical_not(last))
        def _():
            pltpu.make_async_copy(x_held, place, early_sems.at[2 * by + 1]).start()

        pending.append(pltpu.make_async_copy(x_held, place, early_sems.at[2 * by + 1]))
    copies[3].wait()
    copies[7].wait()
    after_self = stream + nn(mix, weights[3][...])
    after_out[...] = after_self
    send(5)
    x_cross = low(after_self * inverse_rms(after_self) * row(gain_cross))
    x_cross_out[...] = x_cross
    send(6)
    copies[8].wait()
    cross_q_out[...] = low(nn(x_cross, weights[4][...]))
    send(7)
    for item in pending:
        item.wait()


def self_forward(call, hidden, cot, gain_self, gain_cross, weights, chips):
    tokens, width = hidden.shape
    low_one = shape(tokens, width)
    args = (hidden, cot, gain_self, gain_cross) + tuple(weights)
    outs = (low_one, low_one, low_one, shape32(tokens, width), shape32(tokens, LANES),
            shape32(tokens, width), low_one, low_one)
    return call(
        functools.partial(self_forward_kernel, chips=chips),
        "self_forward",
        outs + (shape(tokens, 2 * width),) * chips,
        args,
        56,
        [pltpu.VMEM(item.shape, item.dtype) for item in args + outs]
        + [pltpu.VMEM((2, tokens, width), BF)]
        + [pltpu.SemaphoreType.DMA((size,)) for size in (len(args), len(outs), 2 * chips)],
        "i" + "h" * len(args),
    )


def key_values_kernel(encoder, w_ck, w_cv, keys, values, *, block):
    def step(index, carry):
        rows = pl.ds(pl.multiple_of(index * block, block), block)
        here = encoder[rows, :]
        keys[rows, :] = low(nn(here, w_ck[...]))
        values[rows, :] = low(nn(here, w_cv[...]))
        return carry

    lax.fori_loop(0, encoder.shape[0] // block, step, 0)


def key_values(call, encoder, w_ck, w_cv, block):
    return call(
        functools.partial(key_values_kernel, block=block), "key_values", (shape(*encoder.shape), shape(*encoder.shape)), (encoder, w_ck, w_cv), 24, (), "vvv"
    )


def key_rows(ids, count, step):
    key_count = count
    return pl.ds(pl.multiple_of((ids[0] ^ step) * key_count, LANES), key_count)


def cross_forward_kernel(ids, lengths, keys, values, queries, out, *, step, key_count):
    tokens, width = queries.shape
    factor = (width // HEADS) ** -0.5
    rows = key_rows(ids, key_count, step)
    size = (key_count, LANES)
    hidden_key = jnp.where(rows_of(size) < lengths[ids[0] ^ step], 0.0, NEG)
    key_more = jnp.where(lanes_of(size) == LANES - 1, hidden_key, 0.0).astype(BF)
    query_more = last_lane(2 * tokens, 1.0)
    ones = jnp.ones(size, BF)
    pair_width = 2 * width // HEADS
    sums, tops = [], []
    for pair in range(HEADS // 2):
        part = slice(pair * pair_width, (pair + 1) * pair_width)
        mixture, both, top = attend_pair(
            jnp.concatenate([two_heads(queries[:, part] * factor), query_more], 1),
            jnp.concatenate([keys[rows, part], key_more], 1),
            jnp.concatenate([values[rows, part], ones], 1),
        )
        out[:, part] = low(mixture)
        sums.append(both)
        tops.append(top)
    out[:, width:] = low(in_slots(log_totals(sums, tops)))


def cross_forward(call, lengths, queries, keys, values, step, after=(), weight=None):
    tokens, width = queries.shape
    key_count = keys.shape[0] // lengths.shape[0]
    return call(
        functools.partial(cross_forward_kernel, step=step, key_count=key_count),
        "cross_forward", shape(tokens, width + LANES), (lengths, keys, values, queries), 16, (), "isvvv",
        after, weight,
    )


def feed_forward_kernel(
    ids, after_self, cotangent, x_cross, gain_ffn, w_co, w_in, w_out, *refs, count, chips, chunks
):
    packed, refs = refs[:count], refs[count:]
    result_out, grad_after_out, g_cross_out, send_out, grad_gain_out = refs[:5]
    middle = refs[5 : 5 + chips]
    acts, grad_pres, act_held, grad_held = refs[5 + chips :]
    tokens, width = after_self.shape
    units = w_in.shape[1]
    wide = units // chunks
    compact, spread = compact_matrix(), spread_matrix(width)
    logs = [nn(part[:, width:], compact) for part in packed]
    top = functools.reduce(jnp.maximum, logs)
    log_total = top + jnp.log(sum(jnp.exp(item - top) for item in logs))
    mixture = sum(
        nn(low(in_slots(jnp.exp(item - log_total))), spread) * part[:, :width].astype(F32)
        for item, part in zip(logs, packed)
    )
    mix = low(mixture)
    after_cross = after_self[...] + nn(mix, w_co[...])
    x_ffn = low(after_cross * inverse_rms(after_cross) * row(gain_ffn))
    grad_low = cotangent[...]
    slope = (2.0 / 3.141592653589793) ** 0.5
    span = units // chips
    piece = units // (count * chips)

    def step(chunk, carry):
        part = pl.ds(pl.multiple_of(chunk * wide, LANES), wide)
        pre = nn(x_ffn, w_in[:, part])
        square = pre * pre
        bent = jnp.tanh(pre * (slope + (0.044715 * slope) * square))
        act_held[:, part] = low(0.5 * pre * (1.0 + bent))
        grad_act = nt(grad_low, w_out[part, :])
        bend = 0.5 * (1.0 + bent) + 0.5 * pre * (1.0 - bent * bent) * (slope + (3 * 0.044715 * slope) * square)
        grad_held[:, part] = low(grad_act * bend)
        return carry

    lax.fori_loop(0, chunks, step, 0)
    result = after_cross + nn(act_held[...], w_out[...])
    grad_x = nt(grad_held[...], w_in[...])
    for which in range(units // piece):
        slot = which // chips * piece
        acts[which % chips, :, slot : slot + piece] = act_held[:, which * piece : (which + 1) * piece]
    for which in range(chips):
        grad_pres[which] = grad_held[:, which * span : (which + 1) * span]
    result_out[...] = low(result)
    grad_values, grad_gain = norm_back(grad_x, after_cross, row(gain_ffn))
    grad_gain_out[...] = grad_gain
    grad_after = grad_low.astype(F32) + grad_values
    grad_after_out[...] = grad_after
    g_cross = low(grad_after)
    g_cross_out[...] = g_cross
    grad_mix = low(nt(g_cross, w_co[...]))
    delta = head_sums(grad_mix.astype(F32) * mixture, gather_matrix(width))
    send_out[:, :width] = grad_mix
    send_out[:, width:] = low(in_slots(log_total) + in_slots(delta, 3))
    chip = ids[1]
    for by, out in enumerate(middle):
        index = chip ^ by
        out[:, :width] = x_ffn
        out[:, 2 * width : 2 * width + span] = acts[index]
        out[:, 2 * width + span :] = grad_pres[index]
        early = lax.div(index * 2, chips) == 0

        @pl.when(early)
        def _():
            out[:, width : 2 * width] = mix

        @pl.when(jnp.logical_not(early))
        def _():
            out[:, width : 2 * width] = x_cross[...]


def feed_forward(call, after_self, cotangent, x_cross, gain_ffn, w_co, w_in, w_out, packed, chips):
    tokens, width = after_self.shape
    units = w_in.shape[1]
    span, chunks = units // chips, 4
    return call(
        functools.partial(feed_forward_kernel, count=len(packed), chips=chips, chunks=chunks),
        "feed_forward",
        (shape(tokens, width), shape32(tokens, width), shape(tokens, width), shape(tokens, width + LANES),
         shape32(1, width)) + (shape(tokens, 2 * width + 2 * span),) * chips,
        (after_self, cotangent, x_cross, gain_ffn, w_co, w_in, w_out) + tuple(packed),
        28,
        [pltpu.VMEM((chips, tokens, span), BF)] * 2 + [pltpu.VMEM((tokens, units), BF)] * 2,
        "ivvvvvvv" + "v" * len(packed),
    )


def cross_backward_kernel(ids, lengths, keys, values, queries, grads, grad_queries, grad_keys, grad_values, *, step):
    tokens, width = queries.shape
    key_count = grad_keys.shape[0]
    factor = (width // HEADS) ** -0.5
    rows = key_rows(ids, key_count, step)
    size = (key_count, LANES)
    hidden_key = jnp.where(rows_of(size) < lengths[ids[0] ^ step], 0.0, NEG)
    key_more = jnp.where(lanes_of(size) == LANES - 1, hidden_key, minus_slots(key_count, 0)).astype(BF)
    value_more = minus_slots(key_count, 3).astype(BF)
    extra = grads[:, width:]
    one = last_lane(2 * tokens, 1.0)
    pair_width = 2 * width // HEADS
    for pair in range(HEADS // 2):
        part = slice(pair * pair_width, (pair + 1) * pair_width)
        grad_q, grad_k, grad_v = attend_pair_back(
            queries[:, part] * factor, keys[rows, part], values[rows, part], grads[:, part],
            pair_of_slots(extra, pair, 0, one), key_more, pair_of_slots(extra, pair, 3), value_more,
        )
        grad_queries[:, part] = low(grad_q * factor)
        grad_keys[:, part] = low(grad_k)
        grad_values[:, part] = low(grad_v)


def cross_backward(call, lengths, queries, grads, keys, values, step):
    tokens, width = queries.shape
    key_count = keys.shape[0] // lengths.shape[0]
    return call(
        functools.partial(cross_backward_kernel, step=step),
        "cross_backward",
        (shape(tokens, width), shape(key_count, width), shape(key_count, width)),
        (lengths, keys, values, queries, grads), 20, (), "isvvvv",
    )


def extra_rows(four, width):
    return -(-6 * width // four // 8) * 8


def gain_block(gains, four, width_out):
    count = gains.shape[1] // four
    few = extra_rows(four, gains.shape[1])
    high = low(gains).astype(F32)
    rows = [part[i : i + 1, v * four : (v + 1) * four] for part in (high, gains - high) for i in range(3) for v in range(count)]
    block = jnp.concatenate(rows + [jnp.zeros((few - len(rows), four), F32)], 0)
    return low(jnp.concatenate([block, jnp.zeros((few, width_out - four), F32)], 1))


def gain_values(block, four, width):
    count = width // four
    rows = []
    for i in range(3):
        pieces = [
            block[i * count + v : i * count + v + 1, :four] + block[(3 + i) * count + v : (3 + i) * count + v + 1, :four]
            for v in range(count)
        ]
        rows.append(jnp.concatenate(pieces, 1))
    return jnp.concatenate(rows, 0)


def self_backward_kernel(
    ids, grad_after_cross, after_self, hidden, gain_self, gain_cross, grad_gain_ffn, g_cross,
    self_q, self_k, self_v, mixture, logs, *refs, count, chips
):
    weights, partial, refs = refs[:5], refs[5 : 5 + count], refs[5 + count :]
    hidden_out, late = refs[0], refs[1 : 1 + chips]
    fours, twos = refs[1 + chips :]
    tokens, width = after_self.shape
    factor = (width // HEADS) ** -0.5
    four, two = 4 * width // chips, 2 * width // chips
    grad_cq = low(sum(item[...].astype(F32) for item in partial))
    grad_values, grad_gain_cross = norm_back(nt(grad_cq, weights[0][...]), after_self[...], row(gain_cross))
    grad_after = grad_after_cross[...] + grad_values
    g_self = low(grad_after)
    grad_mix = low(nt(g_self, weights[1][...]))
    delta = head_sums(grad_mix.astype(F32) * mixture[...], gather_matrix(width))
    extra = low(in_slots(logs[...]) + in_slots(delta, 3))
    valid = causal_mask(tokens)
    key_more = minus_slots(tokens, 0).astype(BF)
    value_more = minus_slots(tokens, 3).astype(BF)
    pair_width = 2 * width // HEADS
    found = []
    for pair in range(HEADS // 2):
        part = slice(pair * pair_width, (pair + 1) * pair_width)
        grad_q, grad_k, grad_v = attend_pair_back(
            self_q[:, part] * factor, self_k[:, part], self_v[:, part], grad_mix[:, part],
            pair_of_slots(extra, pair, 0), key_more, pair_of_slots(extra, pair, 3), value_more, valid,
        )
        found.append((low(grad_q * factor), low(grad_k), low(grad_v)))
    grads = [jnp.concatenate([item[i] for item in found], 1) for i in range(3)]
    grad_x = jnp.zeros((tokens, width), F32)
    for i in range(3):
        grad_x = grad_x + nt(grads[i], weights[2 + i][...])
    grad_values, grad_gain_self = norm_back(grad_x, hidden[...].astype(F32), row(gain_self))
    hidden_out[...] = low(grad_after + grad_values)
    gains = jnp.concatenate([grad_gain_self, grad_gain_cross, grad_gain_ffn[...]], 0)
    block = gain_block(gains, four, four + two)
    for i, item in enumerate(grads + [g_self]):
        for v in range(width // four):
            fours[i * (width // four) + v] = item[:, v * four : (v + 1) * four]
    for i, item in enumerate((g_cross[...], grad_cq)):
        for v in range(width // two):
            twos[i * (width // two) + v] = item[:, v * two : (v + 1) * two]
    chip = ids[1]
    for by, out in enumerate(late):
        out[:tokens, :four] = fours[chip ^ by]
        out[:tokens, four:] = twos[chip ^ by]
        out[tokens:] = block


def self_backward(call, first, weights, partial, chips):
    tokens, width = first[1].shape
    four, two = 4 * width // chips, 2 * width // chips
    return call(
        functools.partial(self_backward_kernel, count=len(partial), chips=chips),
        "self_backward",
        (shape(tokens, width),) + (shape(tokens + extra_rows(four, width), four + two),) * chips,
        tuple(first) + tuple(weights) + tuple(partial),
        20,
        [pltpu.VMEM((chips, tokens, four), BF), pltpu.VMEM((chips, tokens, two), BF)],
        "i" + "v" * (len(first) + 5 + len(partial)),
    )


def stacked(refs, rows, lanes):
    return jnp.concatenate([item[rows, lanes] for item in refs], 0)


def hand_out(ids, held, keep, give):
    core = ids[2]
    keep[...] = held[core]
    give[...] = held[1 - core]


def ffn_grads_kernel(ids, *refs, chips):
    early, middle, (keep, give, held) = refs[:chips], refs[chips : 2 * chips], refs[2 * chips :]
    _, ring, half, both = held.shape
    span = both // 2
    width = early[0].shape[1] // 2
    every = slice(None)
    grad_in = low(
        tn(stacked(middle, every, slice(0, width)), stacked(middle, every, slice(2 * width + span, 2 * width + 2 * span)))
    )
    for z in range(ring):
        for c in range(2):
            at = (2 * z + c) * half
            held[c, z, :, :span] = grad_in[at : at + half]
    grad_out = low(
        tn(stacked(middle, every, slice(2 * width, 2 * width + span)), stacked(early, every, slice(width, 2 * width)))
    )
    few = span // (2 * ring)
    for z in range(ring):
        for c in range(2):
            at = (2 * z + c) * few
            block = grad_out[at : at + few]
            held[c, z, :, span:] = jnp.concatenate([block[:, v : v + span] for v in range(0, width, span)], 0)
    hand_out(ids, held, keep, give)


def ffn_grads(call, early, middle, ring, units):
    chips = len(early)
    width = early[0].shape[1] // 2
    part = (ring, width // (2 * ring), 2 * units // chips)
    return call(
        functools.partial(ffn_grads_kernel, chips=chips), "ffn_grads", (shape(*part),) * 2,
        tuple(early) + tuple(middle), 28, [pltpu.VMEM((2,) + part, BF)], "i" + "v" * (2 * chips),
    )


def key_grads_kernel(ids, encoder, *refs):
    grads, (keep, give, held) = refs[:-3], refs[-3:]
    count = len(grads) // 2
    _, ring, half, both = held.shape
    width = both // 2
    key_count = grads[0].shape[0]
    rows = jnp.concatenate([encoder[key_rows(ids, key_count, step), :] for step in range(count)], 0)
    for i in range(2):
        grad = low(tn(rows, stacked(grads[i * count : (i + 1) * count], slice(None), slice(None))))
        for z in range(ring):
            for c in range(2):
                at = (2 * z + c) * half
                held[c, z, :, i * width : (i + 1) * width] = grad[at : at + half]
    hand_out(ids, held, keep, give)


def key_grads(call, encoder, grad_keys, grad_values, ring):
    width = encoder.shape[1]
    part = (ring, width // (2 * ring), 2 * width)
    return call(
        key_grads_kernel, "key_grads", (shape(*part),) * 2, (encoder,) + tuple(grad_keys) + tuple(grad_values), 32,
        [pltpu.VMEM((2,) + part, BF)], "iv" + "v" * (2 * len(grad_keys)),
    )


def encoder_grad_kernel(ids, w_ck, w_cv, *refs):
    grads, out, held = refs[:-2], refs[-2], refs[-1]
    count = len(grads) // 2
    key_count = grads[0].shape[0]
    for index, item in enumerate(grads):
        held[index] = item[...]

    def step(index, carry):
        rows = pl.ds(pl.multiple_of((ids[0] ^ index) * key_count, LANES), key_count)
        out[rows, :] = low(nt(held[index], w_ck[...]) + nt(held[count + index], w_cv[...]))
        return carry

    lax.fori_loop(0, count, step, 0)


def encoder_grad(call, w_ck, w_cv, grad_keys, grad_values):
    key_count, width = grad_keys[0].shape
    return call(
        encoder_grad_kernel, "encoder_grad", shape(key_count * len(grad_keys), width),
        (w_ck, w_cv) + tuple(grad_keys) + tuple(grad_values), 12 + 3 * len(grad_keys),
        [pltpu.VMEM((2 * len(grad_keys), key_count, width), BF)], "ivv" + "v" * (2 * len(grad_keys)),
    )


def key_sum_kernel(ids, keep, came, even, odd, held):
    chips, two = held.shape[0], held.shape[3]
    summed = low(keep[...].astype(F32) + came[...].astype(F32))
    for j in range(chips):
        held[j] = summed[:, :, j * two : (j + 1) * two]
    for by in range(chips):
        (even, odd)[by % 2][by // 2] = held[ids[1] ^ by]


def key_sum(call, keep, came, chips):
    ring, half, both = keep.shape
    part = (ring, half, both // chips)
    return call(
        key_sum_kernel, "key_sum", (shape(chips // 2, *part),) * 2, (keep, came), 20, [pltpu.VMEM((chips,) + part, BF)],
        "ivv",
    )


def first_sum_kernel(ids, keep, came, *outs):
    for by in range(keep.shape[0]):
        z = ids[0] ^ by
        outs[by % 2][by // 2] = low(keep[z].astype(F32) + came[z].astype(F32))


def first_sum(call, keep, came):
    part = (keep.shape[0] // 2,) + keep.shape[1:]
    return call(first_sum_kernel, "first_sum", (shape(*part),) * 2, (keep, came), 16, (), "ivv")


def hold_kernel(item, out):
    out[...] = item[...]


def hold(call, item):
    return call(hold_kernel, "hold", shape(*item.shape), (item,), 8, (), "v")


def pack_kernel(*refs):
    for at, item in enumerate(refs[:-1]):
        refs[-1][at] = item[...]


def pack(call, parts):
    return call(pack_kernel, "pack", shape(len(parts), *parts[0].shape), tuple(parts), 16, (), "v" * len(parts))


def add_halves_kernel(*refs, count, inner):
    keep, came, outs = refs[: 1 if inner else count], refs[1 if inner else count], refs[2 if inner else count + 1 :]
    for at in range(count):
        mine = keep[0][at] if inner else keep[at][...]
        outs[at % 2][at // 2] = low(mine.astype(F32) + came[at].astype(F32))


def add_halves(call, name, keep, came):
    inner = not isinstance(keep, (tuple, list))
    count = came.shape[0]
    part = (count // 2,) + came.shape[1:]
    args = (keep,) if inner else tuple(keep)
    return call(
        functools.partial(add_halves_kernel, count=count, inner=inner), name, (shape(*part),) * 2, args + (came,), 16, (),
        "v" * (len(args) + 1),
    )


def halve(call, name, axis, keep, give, by):
    came = swap(give, axis, by)
    if came.shape[0] == 1:
        return keep, came
    keep, give = add_halves(call, name, keep, came)
    return halve(call, name, axis, keep, give, 2 * by)


def tail_grads_kernel(ids, *refs, chips):
    early, middle, late = refs[:chips], refs[chips : 2 * chips], refs[2 * chips : 3 * chips]
    keep, give, held = refs[3 * chips :]
    _, ring, more, both = held.shape
    four = both // 3 * 2
    width = early[0].shape[1] // 2
    half = more - extra_rows(four, width)
    tokens = early[0].shape[0]
    every, rows = slice(None), slice(0, tokens)
    grads = (
        (low(tn(stacked(early, every, slice(0, width)), stacked(late, rows, slice(0, four)))), slice(0, four)),
        (low(tn(stacked(middle, every, slice(width, 2 * width)), stacked(late, rows, slice(four, both)))), slice(four, both)),
    )
    gains = sum(gain_values(item[tokens:].astype(F32), four, width) for item in late)
    block = gain_block(gains, four, both)
    for z in range(ring):
        for c in range(2):
            at = (2 * z + c) * half
            for grad, lanes in grads:
                held[c, z, :half, lanes] = grad[at : at + half]
            held[c, z, half:, :] = block
    hand_out(ids, held, keep, give)


def tail_grads(call, early, middle, late, ring):
    chips = len(early)
    width = early[0].shape[1] // 2
    both = late[0].shape[1]
    part = (ring, width // (2 * ring) + extra_rows(both // 3 * 2, width), both)
    return call(
        functools.partial(tail_grads_kernel, chips=chips), "tail_grads", (shape(*part),) * 2,
        tuple(early) + tuple(middle) + tuple(late), 28, [pltpu.VMEM((2,) + part, BF)], "i" + "v" * (3 * chips),
    )


def tail_sum_kernel(ids, keep, came, part, more, *outs, chips):
    both = keep.shape[2]
    four = both // 3 * 2
    width = four * chips // 4
    half = keep.shape[1] - extra_rows(four, width)
    gains = gain_values(keep[0, half:].astype(F32), four, width) + gain_values(came[0, half:].astype(F32), four, width)
    block = gain_block(gains, four, outs[0].shape[1])
    for by, out in enumerate(outs):
        z = ids[0] ^ by
        out[:half, :both] = low(keep[z, :half].astype(F32) + came[z, :half].astype(F32))
        out[:half, both:] = low(part[0, z].astype(F32) + more[0, z].astype(F32))
        out[half:] = block


def tail_sum(call, keep, came, parts, chips):
    ring, more, both = keep.shape
    return call(
        functools.partial(tail_sum_kernel, chips=chips), "tail_sum",
        (shape(more, both + parts[0].shape[3]),) * ring, (keep, came) + tuple(parts), 16, (), "ivvvv",
    )


def ring_sum_kernel(keep, came, out):
    out[...] = low(keep[0].astype(F32) + came[0].astype(F32))


def ring_sum(call, parts):
    return call(ring_sum_kernel, "ring_sum", shape(*parts[0].shape[1:]), tuple(parts), 16, (), "vv")


def last_sum_kernel(ids, *refs):
    parts, (out, gains_out, held) = refs[:-3], refs[-3:]
    half, both = out.shape
    ring, _, rows = held.shape
    four = both // 2
    out[...] = low(sum(item[:half].astype(F32) for item in parts))
    gains = sum(gain_values(item[half:].astype(F32), four, ring * rows) for item in parts)
    for z in range(ring):
        held[z] = gains[:, z * rows : (z + 1) * rows]
    gains_out[...] = held[ids[0]]


def last_sum(call, parts, rows):
    more, both = parts[0].shape
    half = rows // 2
    return call(
        last_sum_kernel, "last_sum", (shape(half, both), shape32(3, rows)), tuple(parts), 16,
        [pltpu.VMEM((len(parts), 3, rows), F32)], "i" + "v" * len(parts),
    )


def place_pieces(ids, own, other, held):
    for by in range(own.shape[0]):
        held[ids[1] ^ by, ids[2]] = own[by]
        held[ids[1] ^ by, 1 - ids[2]] = other[by]


def first_out_kernel(ids, *refs, chips):
    own, other, in_out, out_out, held = refs
    place_pieces(ids, own, other, held)
    half, wide = held.shape[2:]
    span = wide // 2
    width = out_out.shape[1]
    few = half * span // width
    for j in range(chips):
        for c in range(2):
            rows = slice(c * half, (c + 1) * half)
            in_out[rows, j * span : (j + 1) * span] = held[j, c, :, :span].astype(F32)
            for v in range(width // span):
                at = (2 * j + c) * few
                out_out[at : at + few, v * span : (v + 1) * span] = held[
                    j, c, v * few : (v + 1) * few, span : 2 * span
                ].astype(F32)


def first_out(call, own, other, units, width):
    chips, half, wide = own.shape
    rows = 2 * half
    return call(
        functools.partial(first_out_kernel, chips=chips), "first_out",
        (shape32(rows, units), shape32(rows * units // width, width)),
        (own, other), 24, [pltpu.VMEM((chips, 2, half, wide), BF)], "ivv",
    )


def last_out_kernel(ids, *refs, chips):
    own, other, outs, held = refs[0], refs[1], refs[2:-1], refs[-1]
    place_pieces(ids, own, other, held)
    half, both = held.shape[2:]
    four, two = both // 2, both // 4
    for j in range(chips):
        for c in range(2):
            rows = slice(c * half, (c + 1) * half)
            at = j % (chips // 4) * four
            outs[j * 4 // chips][rows, at : at + four] = held[j, c, :, :four].astype(F32)
            at = j % (chips // 2) * two
            outs[4 + j * 2 // chips][rows, at : at + two] = held[j, c, :, four : four + two].astype(F32)
            outs[6 + j * 2 // chips][rows, at : at + two] = held[j, c, :, four + two :].astype(F32)


def last_out(call, own, other, width):
    chips, half, both = own.shape
    return call(
        functools.partial(last_out_kernel, chips=chips), "last_out", (shape32(2 * half, width),) * 8,
        (own, other), 24, [pltpu.VMEM((chips, 2, half, both), BF)], "ivv",
    )


def swap(values, axis, by):
    peers = lax.axis_size(axis)
    return lax.ppermute(values, axis, [(i, i ^ by) for i in range(peers)])


def over_chips(blocks):
    return [blocks[0]] + [swap(item, "pb", 2 * by) for by, item in enumerate(blocks) if by]


def over_ring(blocks):
    return [blocks[0]] + [swap(item, "pa", by) for by, item in enumerate(blocks) if by]


def over_core(blocks):
    return [swap(item, "pb", 1) for item in blocks]


def body(
    hidden, encoder, lengths, w_sq, w_sk, w_sv, w_so, w_cq, w_ck, w_cv, w_co, w_in, w_out,
    gain_self, gain_cross, gain_ffn, cotangent,
):
    _, tokens, width = hidden.shape
    questions, _, passage_len, _ = encoder.shape
    units = w_in.shape[1]
    ring = lax.axis_size("pa")
    chips = lax.axis_size("pb") // 2
    true_len = lengths.reshape(questions)
    hidden2 = hidden.reshape(tokens, width)
    cot = cotangent.reshape(tokens, width)
    enc = encoder.reshape(questions * passage_len, width)

    call = Line()
    found = self_forward(call, hidden2, cot, gain_self, gain_cross, (w_sq, w_sk, w_sv, w_so, w_cq), chips)
    self_q, self_k, self_v, mixture, logs, after_self, x_cross, cross_q = found[:8]
    asked = over_ring([cross_q] * ring)
    early = over_chips(found[8:])
    keys, values = key_values(call, enc, w_ck, w_cv, passage_len)
    near = chips - 1
    partial = []
    for step in range(ring):
        last = step == ring - 1
        partial.append(
            cross_forward(call, true_len, asked[step], keys, values, step, early[1:near] if last else (), 10 if last else None)
        )
    packed = over_ring(partial)
    call.meet(0, packed[1 : ring - 1] + early[near:])
    call.meet(3)
    found = feed_forward(call, after_self, cot, x_cross, gain_ffn, w_co, w_in, w_out, packed, chips)
    result, grad_after_cross, g_cross, sent, grad_gain_ffn = found[:5]
    given = over_ring([sent] * ring)
    middle = list(found[5:])
    back = {}
    for step in range(ring):
        back[step] = cross_backward(call, true_len, asked[step], given[step], keys, values, step)
        if step == 0:
            middle[near] = hold(call, middle[near])
    middle = over_chips(middle)
    partial = over_ring([back[step][0] for step in range(ring)])
    grad_keys, grad_values = [back[step][1] for step in range(ring)], [back[step][2] for step in range(ring)]
    key_keep, key_give = key_grads(call, enc, grad_keys, grad_values, ring)
    grad_encoder = encoder_grad(call, w_ck, w_cv, grad_keys, grad_values)
    ffn_keep, ffn_give = ffn_grads(call, early, middle, ring, units)
    call.meet(0, partial[2:])
    call.meet(20, ())
    key_parts = key_sum(call, key_keep, swap(key_give, "pb", 1), chips)
    first = first_sum(call, ffn_keep, swap(ffn_give, "pb", 1))
    found = self_backward(
        call,
        (grad_after_cross, after_self, hidden2, gain_self, gain_cross, grad_gain_ffn, g_cross,
         self_q, self_k, self_v, mixture, logs),
        (w_cq, w_so, w_sq, w_sk, w_sv),
        partial,
        chips,
    )
    grad_hidden = found[0]
    late = over_chips(found[1:])
    key_parts = halve(call, "key_add", "pb", *key_parts, 2)
    first = halve(call, "first_add", "pa", *first, 1)
    keep, give = tail_grads(call, early, middle, late, ring)
    call.meet(0, [key_parts[1], first[1]])
    call.meet(12)
    last = over_ring(tail_sum(call, keep, swap(give, "pb", 1), key_parts, chips))
    first = over_chips([ring_sum(call, first)] * chips)
    last, gains = last_sum(call, last, width // ring)
    last = over_chips([last] * chips)
    first = pack(call, first)
    last = pack(call, last)
    grad_in, grad_out = first_out(call, first, swap(first, "pb", 1), units, width)
    grad_sq, grad_sk, grad_sv, grad_so, grad_co, grad_cq, grad_ck, grad_cv = last_out(
        call, last, swap(last, "pb", 1), width
    )
    return (
        result.reshape(hidden.shape),
        grad_hidden.reshape(hidden.shape),
        grad_encoder.reshape(encoder.shape),
        grad_sq,
        grad_sk,
        grad_sv,
        grad_so,
        grad_cq,
        grad_ck,
        grad_cv,
        grad_co,
        grad_in,
        grad_out,
        gains[0],
        gains[1],
        gains[2],
    )


def solution(mesh):
    split = P(("pb", "pa"), None, None)
    passages = P("pb", "pa", None, None)
    return jax.shard_map(
        body,
        mesh=mesh,
        in_specs=(split, passages, P("pb", "pa")) + (P(),) * 13 + (split,),
        out_specs=(split, split, passages) + (P("pa", None),) * 10 + (P("pa"),) * 3,
        check_vma=False,
    )
```

time: 285 us -> 196 us (0.69); the launches traced: 285 us -> 193 us
  waiting for transfers between devices: 131 us -> 76.9 us
  starting transfers between devices: 66.7 us -> 47 us
  local copies, waits for them, and re-layouts: 15.7 us -> 1.83 us
  matrix products: 9.73 us -> 0 us
  Pallas kernels: 60.1 us -> 65.4 us
    ppermute x18 -> x0, waiting for transfers between devices: 89.9 us -> none  [shift(): lax.ppermute(values, axis, [(i, (i + by) % peers) for i in range(peers)])]
    ppermute x29 -> x39, waiting for transfers between devices: 41.3 us -> 76.9 us  [swap(): return lax.ppermute(values, axis, [(i, i ^ by) for i in range(peers)])]
    ppermute x18 -> x0, starting transfers between devices: 22.4 us -> none  [shift(): lax.ppermute(values, axis, [(i, (i + by) % peers) for i in range(peers)])]
    unnamed x74 -> x60, local copies, waits for them, and re-layouts: 13.7 us -> 1.26 us
    dot_general x4 -> x0, matrix products: 9.73 us -> none  [dot(): lax.dot_general(left, right, (((left_dim,), (right_dim,)), ((), ())), pre...]
    pallas_call x15 -> x34, Pallas kernels: 60.1 us -> 65.4 us  [__call__(): pl.pallas_call(run, out_shape=outs, in_specs=specs + [pl.BlockSpec(memory...]
    ppermute x29 -> x39, starting transfers between devices: 44.2 us -> 47 us  [swap(): return lax.ppermute(values, axis, [(i, i ^ by) for i in range(peers)])]
  transfers between devices with their start and end apart: 47 -> 39, of which waited for: 24 -> 15; matrix products, arithmetic and copies ran while one was open for 4% -> 0% of each run, Pallas kernels for 11% -> 25%
where the time goes in v1:
time: 196 us; the launch traced here: 193 us
  waiting for transfers between devices  76.9 us (39%)
  Pallas kernels  65.4 us (33%)
  starting transfers between devices  47 us (24%)
    ppermute x39, waiting for transfers between devices, swap(): return lax.ppermute(values, axis, [(i, i ^ by) for i in range(peers)])  76.9 us
    pallas_call x34, Pallas kernels, __call__(): pl.pallas_call(run, out_shape=outs, in_specs=specs + [pl.BlockSpec(memory...  65.4 us
    ppermute x39, starting transfers between devices, swap(): return lax.ppermute(values, axis, [(i, i ^ by) for i in range(peers)])  47 us
  transfers between devices with their start and end apart: 39, of which 15 were waited for; matrix products, arithmetic and copies ran while one was open for 0% of the time, Pallas kernels for 25%

profile of v1, /device:TPU:9, one launch (start us, length us, event | category | flops | bytes accessed | tf_op | source)
XLA Modules:
  0.0 192.8 jit_solution(1584873991577288500)
XLA Ops:
  0.7 6.3 %self_forward.1 = (bf16[128,768]{1,0:T(8,128)(2,1)}, bf16[128,768]{1,0:T(8,128)(2,1)}, bf16[128,768]{1,0:T(8,128)(2,1)}, f32[128,768]{1,0:T(8,128)}, f32[128,128...) custom-call(bf16[128,768]{1,0:T(8,128)(2,1)} %bitcast.14, ...), custom_call_target="tpu_custom_call" | custom-call | tf_op jit(solution)/shard_map/self_forward/pallas_call | solution.py:232
  7.0 1.4 collective-permute-start.4
  13.7 4.5 %key_values.1 = (bf16[1536,768]{1,0:T(8,128)(2,1)S(1)}, bf16[1536,768]{1,0:T(8,128)(2,1)S(1)}, f32[8,128]{1,0:T(8,128)S(1)}) custom-call(bf16[1536,768]{1,0:T(8,128)(2,1)S(1)} %bitcast.28, bf16[768,768]{1,0:T(8,128)(2,1)S(1)} %copy-done.1, bf16[768,768]{1,0:T(8,128)(2,1)S(1)} %copy-done.2, f32[8,128]{1,0:T(8,128)S(1)} %copy-done.24), custom_call_target="tpu_custom_call" | custom-call | flops 5765000192 | tf_op jit(solution)/shard_map/key_values/pallas_call | solution.py:232
  18.2 2.0 %cross_forward.4 = (bf16[128,896]{1,0:T(8,128)(2,1)S(1)}, f32[8,128]{1,0:T(8,128)S(1)}) custom-call(s32[4]{0:T(128)S(1)} %bitcast.16, bf16[1536,768]{1,0:T(8,128)(2,1)S(1)} %get-tuple-element.125.refs_1_, bf16[1536,768]{1,0:T(8,128)(2,1)S(1)} %get-tuple-element.126.refs_2_, bf16[128,768]{1,0:T(8,128)(2,1)S(1)} %copy-done.8, ...), custom_call_target="tpu_custom_call" | custom-call | flops 1152999936 | tf_op jit(solution)/shard_map/cross_forward/pallas_call | solution.py:232
  20.2 3.4 %collective-permute-done.refs_3_ = bf16[128,768]{1,0:T(8,128)(2,1)S(1)} collective-permute-done((bf16[128,768]{1,0:T(8,128)(2,1)}, bf16[128,768]{1,0:T(8,128)(2,1)S(1)}, u32[]{:S(2)}, u32[]{:S(2)}) %collective-permute-start) | collective-permute-done | bytes 196640 | tf_op jit(solution)/shard_map/ppermute | solution.py:944
  23.6 2.2 %collective-permute-start.8 = (bf16[128,1536]{1,0:T(8,128)(2,1)S(1)}, bf16[128,1536]{1,0:T(8,128)(2,1)S(1)}, u32[]{:S(2)}, u32[]{:S(2)}) collective-permute-start(bf16[128,1536]{1,0:T(8,128)(2,1)S(1)} %copy-done.25), channel_id=1, source_target_pairs={{0,24},{4,28},{8,16},{12,20},{16,8},{20,12},{24,0},{28,4},{1,25},{... | collective-permute-start | bytes 1179656 | tf_op jit(solution)/shard_map/ppermute | solution.py:944
  25.8 2.0 %cross_forward.5 = (bf16[128,896]{1,0:T(8,128)(2,1)S(1)}, f32[8,128]{1,0:T(8,128)S(1)}) custom-call(s32[4]{0:T(128)S(1)} %bitcast.17, bf16[1536,768]{1,0:T(8,128)(2,1)S(1)} %get-tuple-element.125.refs_1_, bf16[1536,768]{1,0:T(8,128)(2,1)S(1)} %get-tuple-element.126.refs_2_, bf16[128,768]{1,0:T(8,128)(2,1)S(1)} %collective-permute-done.refs_3_, ...), custom_call_target="tpu_custom_call" | custom-call | flops 1152999936 | tf_op jit(solution)/shard_map/cross_forward/pallas_call | solution.py:232
  27.8 2.0 %cross_forward.6 = (bf16[128,896]{1,0:T(8,128)(2,1)S(1)}, f32[8,128]{1,0:T(8,128)S(1)}) custom-call(s32[4]{0:T(128)S(1)} %bitcast.18, bf16[1536,768]{1,0:T(8,128)(2,1)S(1)} %get-tuple-element.125.refs_1_, bf16[1536,768]{1,0:T(8,128)(2,1)S(1)} %get-tuple-element.126.refs_2_, bf16[128,768]{1,0:T(8,128)(2,1)S(1)} %collective-permute-done.2.refs_3_, ...), custom_call_target="tpu_custom_call" | custom-call | flops 1152999936 | tf_op jit(solution)/shard_map/cross_forward/pallas_call | solution.py:232
  30.3 2.0 %cross_forward.7 = (bf16[128,896]{1,0:T(8,128)(2,1)S(1)}, f32[8,128]{1,0:T(8,128)S(1)}) custom-call(s32[4]{0:T(128)S(1)} %bitcast.19, bf16[1536,768]{1,0:T(8,128)(2,1)S(1)} %get-tuple-element.125.refs_1_, bf16[1536,768]{1,0:T(8,128)(2,1)S(1)} %get-tuple-element.126.refs_2_, bf16[128,768]{1,0:T(8,128)(2,1)S(1)} %collective-permute-done.4.refs_3_, ...), custom_call_target="tpu_custom_call" | custom-call | flops 11530000384 | tf_op jit(solution)/shard_map/cross_forward/pallas_call | solution.py:232
  32.4 2.4 %collective-permute-start.7 = (bf16[128,896]{1,0:T(8,128)(2,1)S(1)}, bf16[128,896]{1,0:T(8,128)(2,1)S(1)}, u32[]{:S(2)}, u32[]{:S(2)}) collective-permute-start(bf16[128,896]{1,0:T(8,128)(2,1)S(1)} %get-tuple-element.137), channel_id=1, source_target_pairs={{0,3},{1,2},{2,1},{3,0},{4,7},{5,6},{6,5},{7,4},{8,11},{9,10},{10,... | collective-permute-start | bytes 688136 | tf_op jit(solution)/shard_map/ppermute | solution.py:944
  34.7 6.9 %collective-permute-done.3.refs_2_.refs_9_ = bf16[128,896]{1,0:T(8,128)(2,1)S(1)} collective-permute-done((bf16[128,896]{1,0:T(8,128)(2,1)S(1)}, bf16[128,896]{1,0:T(8,128)(2,1)S(1)}, u32[]{:S(2)}, u32[]{:S(2)}) %collective-permute-start.3) | collective-permute-done | bytes 229408 | tf_op jit(solution)/shard_map/ppermute | solution.py:944
  41.7 8.3 %collective-permute-done.7.refs_10_ = bf16[128,896]{1,0:T(8,128)(2,1)S(1)} collective-permute-done((bf16[128,896]{1,0:T(8,128)(2,1)S(1)}, bf16[128,896]{1,0:T(8,128)(2,1)S(1)}, u32[]{:S(2)}, u32[]{:S(2)}) %collective-permute-start.7) | collective-permute-done | bytes 229408 | tf_op jit(solution)/shard_map/ppermute | solution.py:944
  50.1 8.8 %feed_forward.1 = (bf16[128,768]{1,0:T(8,128)(2,1)}, f32[128,768]{1,0:T(8,128)S(1)}, bf16[128,768]{1,0:T(8,128)(2,1)S(1)}, bf16[128,896]{1,0:T(8,128)(2,1)S(1)},...) custom-call(f32[128,768]{1,0:T(8,128)S(1)} %copy-done.17, ...), custom_call_target="tpu_custom_call" | custom-call | flops 5765000192 | tf_op jit(solution)/shard_map/feed_forward/pallas_call | solution.py:232
  58.9 3.4 %collective-permute-start.11 = (bf16[128,896]{1,0:T(8,128)(2,1)S(1)}, bf16[128,896]{1,0:T(8,128)(2,1)S(1)}, u32[]{:S(2)}, u32[]{:S(2)}) collective-permute-start(bf16[128,896]{1,0:T(8,128)(2,1)S(1)} %get-tuple-element.149.refs_4_), channel_id=1, source_target_pairs={{0,2},{1,3},{2,0},{3,1},{4,6},{5,7},{6,4},{7,5},{8,10},{9,11},{10,... | collective-permute-start | bytes 688136 | tf_op jit(solution)/shard_map/ppermute | solution.py:944
  62.8 2.2 %collective-permute-start.16 = (bf16[128,3072]{1,0:T(8,128)(2,1)S(1)}, bf16[128,3072]{1,0:T(8,128)(2,1)S(1)}, u32[]{:S(2)}, u32[]{:S(2)}) collective-permute-start(bf16[128,3072]{1,0:T(8,128)(2,1)S(1)} %get-tuple-element.163), channel_id=1, source_target_pairs={{0,16},{4,20},{8,24},{12,28},{16,0},{20,4},{24,8},{28,12},{1,17},{... | collective-permute-start | bytes 2359304 | tf_op jit(solution)/shard_map/ppermute | solution.py:944
  65.1 2.8 %cross_backward.4 = (bf16[128,768]{1,0:T(8,128)(2,1)S(1)}, bf16[384,768]{1,0:T(8,128)(2,1)S(1)}, bf16[384,768]{1,0:T(8,128)(2,1)S(1)}, f32[8,128]{1,0:T(8,128)S(1)}) custom-call(s32[4]{0:T(128)S(1)} %bitcast.20, bf16[1536,768]{1,0:T(8,128)(2,1)S(1)} %get-tuple-element.125.refs_1_, bf16[1536,768]{1,0:T(8,128)(2,1)S(1)} %get-tuple-element.126.refs_2_, ...), custom_call_target="tpu_custom_call" | custom-call | tf_op jit(solution)/shard_map/cross_backward/pallas_call | solution.py:232
  67.9 2.6 %collective-permute-start.17 = (bf16[128,3072]{1,0:T(8,128)(2,1)S(1)}, bf16[128,3072]{1,0:T(8,128)(2,1)S(1)}, u32[]{:S(2)}, u32[]{:S(2)}) collective-permute-start(bf16[128,3072]{1,0:T(8,128)(2,1)S(1)} %get-tuple-element.164), channel_id=1, source_target_pairs={{0,24},{4,28},{8,16},{12,20},{16,8},{20,12},{24,0},{28,4},{1,25},{... | collective-permute-start | bytes 2359304 | tf_op jit(solution)/shard_map/ppermute | solution.py:944
  70.5 2.8 %cross_backward.5 = (bf16[128,768]{1,0:T(8,128)(2,1)S(1)}, bf16[384,768]{1,0:T(8,128)(2,1)S(1)}, bf16[384,768]{1,0:T(8,128)(2,1)S(1)}, f32[8,128]{1,0:T(8,128)S(1)}) custom-call(s32[4]{0:T(128)S(1)} %bitcast.21, bf16[1536,768]{1,0:T(8,128)(2,1)S(1)} %get-tuple-element.125.refs_1_, bf16[1536,768]{1,0:T(8,128)(2,1)S(1)} %get-tuple-element.126.refs_2_, ...), custom_call_target="tpu_custom_call" | custom-call | tf_op jit(solution)/shard_map/cross_backward/pallas_call | solution.py:232
  73.3 3.4 %collective-permute-done.11.refs_4_ = bf16[128,896]{1,0:T(8,128)(2,1)S(1)} collective-permute-done((bf16[128,896]{1,0:T(8,128)(2,1)S(1)}, bf16[128,896]{1,0:T(8,128)(2,1)S(1)}, u32[]{:S(2)}, u32[]{:S(2)}) %collective-permute-start.11) | collective-permute-done | bytes 229408 | tf_op jit(solution)/shard_map/ppermute | solution.py:944
  76.7 2.8 %cross_backward.6 = (bf16[128,768]{1,0:T(8,128)(2,1)S(1)}, bf16[384,768]{1,0:T(8,128)(2,1)S(1)}, bf16[384,768]{1,0:T(8,128)(2,1)S(1)}, f32[8,128]{1,0:T(8,128)S(1)}) custom-call(s32[4]{0:T(128)S(1)} %bitcast.22, bf16[1536,768]{1,0:T(8,128)(2,1)S(1)} %get-tuple-element.125.refs_1_, bf16[1536,768]{1,0:T(8,128)(2,1)S(1)} %get-tuple-element.126.refs_2_, ...), custom_call_target="tpu_custom_call" | custom-call | tf_op jit(solution)/shard_map/cross_backward/pallas_call | solution.py:232
  79.4 2.1 %collective-permute-done.13.refs_4_ = bf16[128,896]{1,0:T(8,128)(2,1)S(1)} collective-permute-done((bf16[128,896]{1,0:T(8,128)(2,1)S(1)}, bf16[128,896]{1,0:T(8,128)(2,1)S(1)}, u32[]{:S(2)}, u32[]{:S(2)}) %collective-permute-start.13) | collective-permute-done | bytes 229408 | tf_op jit(solution)/shard_map/ppermute | solution.py:944
  81.6 2.8 %cross_backward.7 = (bf16[128,768]{1,0:T(8,128)(2,1)S(1)}, bf16[384,768]{1,0:T(8,128)(2,1)S(1)}, bf16[384,768]{1,0:T(8,128)(2,1)S(1)}, f32[8,128]{1,0:T(8,128)S(1)}) custom-call(s32[4]{0:T(128)S(1)} %bitcast.23, bf16[1536,768]{1,0:T(8,128)(2,1)S(1)} %get-tuple-element.125.refs_1_, bf16[1536,768]{1,0:T(8,128)(2,1)S(1)} %get-tuple-element.126.refs_2_, ...), custom_call_target="tpu_custom_call" | custom-call | tf_op jit(solution)/shard_map/cross_backward/pallas_call | solution.py:232
  84.3 2.3 %collective-permute-start.14 = (bf16[128,768]{1,0:T(8,128)(2,1)S(1)}, bf16[128,768]{1,0:T(8,128)(2,1)S(1)}, u32[]{:S(2)}, u32[]{:S(2)}) collective-permute-start(bf16[128,768]{1,0:T(8,128)(2,1)S(1)} %get-tuple-element.159), channel_id=1, source_target_pairs={{0,3},{1,2},{2,1},{3,0},{4,7},{5,6},{6,5},{7,4},{8,11},{9,10},{10,... | collective-permute-start | bytes 589832 | tf_op jit(solution)/shard_map/ppermute | solution.py:944
  86.6 4.1 %key_grads.1 = (bf16[4,96,1536]{2,1,0:T(8,128)(2,1)S(1)}, bf16[4,96,1536]{2,1,0:T(8,128)(2,1)S(1)}, f32[8,128]{1,0:T(8,128)S(1)}) custom-call(bf16[1536,768]{1,0:T(8,128)(2,1)S(1)} %bitcast.29, bf16[384,768]{1,0:T(8,128)(2,1)S(1)} %get-tuple-element.165.refs_1_.refs_2_, bf16[384,768]{1,0:T(8,128)(2,1)S(1)} %get-tuple-element.166.refs_2_.refs_3_, ...), custom_call_target="tpu_custom_call" | custom-call | flops 6918000128 | tf_op jit(solution)/shard_map/key_grads/pallas_call | solution.py:232
  90.7 6.4 %encoder_grad.1 = (bf16[1536,768]{1,0:T(8,128)(2,1)}, f32[8,128]{1,0:T(8,128)S(1)}) custom-call(bf16[768,768]{1,0:T(8,128)(2,1)S(1)} %copy-done.1, bf16[768,768]{1,0:T(8,128)(2,1)S(1)} %copy-done.2, bf16[384,768]{1,0:T(8,128)(2,1)S(1)} %get-tuple-element.165.refs_1_.refs_2_, bf16[384,768]{1,0:T(8,128)(2,1)S(1)} %get-tuple-element.166.refs_2_.refs_3_, ...), custom_call_target="tpu_custom_call" | custom-call | tf_op jit(solution)/shard_map/encoder_grad/pallas_call | solution.py:232
  98.4 2.1 %collective-permute-start.19 = (bf16[4,96,1536]{2,1,0:T(8,128)(2,1)S(1)}, bf16[4,96,1536]{2,1,0:T(8,128)(2,1)S(1)}, u32[]{:S(2)}, u32[]{:S(2)}) collective-permute-start(bf16[4,96,1536]{2,1,0:T(8,128)(2,1)S(1)} %get-tuple-element.179), channel_id=1, source_target_pairs={{0,4},{4,0},{8,12},{12,8},{16,20},{20,16},{24,28},{28,24},{1,5},{5... | collective-permute-start | bytes 3538952 | tf_op jit(solution)/shard_map/ppermute | solution.py:944
  100.4 1.7 ffn_grads.1
  102.2 1.4 collective-permute-done.12.refs_1_.refs_19_
  104.4 1.5 collective-permute-start.24
  107.6 5.6 %self_backward.1 = (bf16[128,768]{1,0:T(8,128)(2,1)}, bf16[136,1152]{1,0:T(8,128)(2,1)S(1)}, bf16[136,1152]{1,0:T(8,128)(2,1)S(1)}, bf16[136,1152]{1,0:T(8,128)(...) custom-call(f32[128,768]{1,0:T(8,128)S(1)} %get-tuple-element.141.refs_0_, f32[128,768]{1,0:T(8,128)S(1)} %copy-done.17, ...), custom_call_target="tpu_custom_call" | custom-call | flops 23060000768 | tf_op jit(solution)/shard_map/self_backward/pallas_call | solution.py:232
  116.2 2.7 %collective-permute-done.24.refs_1_ = bf16[2,4,96,384]{3,2,1,0:T(8,128)(2,1)S(1)} collective-permute-done((bf16[2,4,96,384]{3,2,1,0:T(8,128)(2,1)S(1)}, bf16[2,4,96,384]{3,2,1,0:T(8,128)(2,1)S(1)}, u32[]{:S(2)}, u32[]{:S(2)}) %collective-permute-start.24) | collective-permute-done | bytes 589856 | tf_op jit(solution)/shard_map/ppermute | solution.py:944
  119.1 1.7 collective-permute-start.26
  120.9 1.7 collective-permute-start.27
  122.6 3.1 %collective-permute-done.20.refs_9_ = bf16[136,1152]{1,0:T(8,128)(2,1)S(1)} collective-permute-done((bf16[136,1152]{1,0:T(8,128)(2,1)S(1)}, bf16[136,1152]{1,0:T(8,128)(2,1)S(1)}, u32[]{:S(2)}, u32[]{:S(2)}) %collective-permute-start.20) | collective-permute-done | bytes 313376 | tf_op jit(solution)/shard_map/ppermute | solution.py:944
  125.6 8.1 %collective-permute-done.22.refs_11_ = bf16[136,1152]{1,0:T(8,128)(2,1)S(1)} collective-permute-done((bf16[136,1152]{1,0:T(8,128)(2,1)S(1)}, bf16[136,1152]{1,0:T(8,128)(2,1)S(1)}, u32[]{:S(2)}, u32[]{:S(2)}) %collective-permute-start.22) | collective-permute-done | bytes 313376 | tf_op jit(solution)/shard_map/ppermute | solution.py:944
  133.7 1.7 tail_grads.1
  136.7 2.1 %collective-permute-done.25.refs_1_ = bf16[4,104,1152]{2,1,0:T(8,128)(2,1)S(1)} collective-permute-done((bf16[4,104,1152]{2,1,0:T(8,128)(2,1)S(1)}, bf16[4,104,1152]{2,1,0:T(8,128)(2,1)S(1)}, u32[]{:S(2)}, u32[]{:S(2)}) %collective-permute-start.25) | collective-permute-done | bytes 958496 | tf_op jit(solution)/shard_map/ppermute | solution.py:944
  139.1 1.5 collective-permute-start.28
  140.6 1.4 collective-permute-start.29
  144.7 8.9 %collective-permute-done.28.refs_1_ = bf16[104,1536]{1,0:T(8,128)(2,1)S(1)} collective-permute-done((bf16[104,1536]{1,0:T(8,128)(2,1)S(1)}, bf16[104,1536]{1,0:T(8,128)(2,1)S(1)}, u32[]{:S(2)}, u32[]{:S(2)}) %collective-permute-start.28) | collective-permute-done | bytes 319520 | tf_op jit(solution)/shard_map/ppermute | solution.py:944
  154.2 7.7 %collective-permute-done.29.refs_2_ = bf16[104,1536]{1,0:T(8,128)(2,1)S(1)} collective-permute-done((bf16[104,1536]{1,0:T(8,128)(2,1)S(1)}, bf16[104,1536]{1,0:T(8,128)(2,1)S(1)}, u32[]{:S(2)}, u32[]{:S(2)}) %collective-permute-start.29) | collective-permute-done | bytes 319520 | tf_op jit(solution)/shard_map/ppermute | solution.py:944
  161.9 7.7 %collective-permute-done.30.refs_3_ = bf16[104,1536]{1,0:T(8,128)(2,1)S(1)} collective-permute-done((bf16[104,1536]{1,0:T(8,128)(2,1)S(1)}, bf16[104,1536]{1,0:T(8,128)(2,1)S(1)}, u32[]{:S(2)}, u32[]{:S(2)}) %collective-permute-start.30) | collective-permute-done | bytes 319520 | tf_op jit(solution)/shard_map/ppermute | solution.py:944
  170.9 1.8 collective-permute-start.32
  172.9 2.1 %collective-permute-start.38 = (bf16[4,96,1536]{2,1,0:T(8,128)(2,1)S(1)}, bf16[4,96,1536]{2,1,0:T(8,128)(2,1)S(1)}, u32[]{:S(2)}, u32[]{:S(2)}) collective-permute-start(bf16[4,96,1536]{2,1,0:T(8,128)(2,1)S(1)} %get-tuple-element.214.refs_0_), channel_id=1, source_target_pairs={{0,4},{4,0},{8,12},{12,8},{16,20},{20,16},{24,28},{28,24},{1,5},{5... | collective-permute-start | bytes 3538952 | tf_op jit(solution)/shard_map/ppermute | solution.py:944
  175.0 3.0 %collective-permute-done.33.refs_3_ = bf16[96,1536]{1,0:T(8,128)(2,1)S(1)} collective-permute-done((bf16[96,1536]{1,0:T(8,128)(2,1)S(1)}, bf16[96,1536]{1,0:T(8,128)(2,1)S(1)}, u32[]{:S(2)}, u32[]{:S(2)}) %collective-permute-start.33) | collective-permute-done | bytes 294944 | tf_op jit(solution)/shard_map/ppermute | solution.py:944
  178.0 8.1 %collective-permute-done.32.refs_2_ = bf16[96,1536]{1,0:T(8,128)(2,1)S(1)} collective-permute-done((bf16[96,1536]{1,0:T(8,128)(2,1)S(1)}, bf16[96,1536]{1,0:T(8,128)(2,1)S(1)}, u32[]{:S(2)}, u32[]{:S(2)}) %collective-permute-start.32) | collective-permute-done | bytes 294944 | tf_op jit(solution)/shard_map/ppermute | solution.py:944
  187.3 2.6 %first_out.1 = (f32[192,3072]{1,0:T(8,128)}, f32[768,768]{1,0:T(8,128)}, f32[8,128]{1,0:T(8,128)S(1)}) custom-call(bf16[4,96,1536]{2,1,0:T(8,128)(2,1)S(1)} %get-tuple-element.214.refs_0_, bf16[4,96,1536]{2,1,0:T(8,128)(2,1)S(1)} %collective-permute-done.38.refs_1_, f32[8,128]{1,0:T(8,128)S(1)} %get-tuple-element.215.refs_2_), custom_call_target="tpu_custom_call" | custom-call | tf_op jit(solution)/shard_map/first_out/pallas_call | solution.py:232
  190.0 2.4 %last_out.1 = (f32[192,768]{1,0:T(8,128)}, f32[192,768]{1,0:T(8,128)}, f32[192,768]{1,0:T(8,128)}, f32[192,768]{1,0:T(8,128)}, f32[192,768]{1,0:T(8,128)}, /*ind...) custom-call(bf16[4,96,1536]{2,1,0:T(8,128)(2,1)S(1)} %get-tuple-element.213.refs_0_, ...), custom_call_target="tpu_custom_call" | custom-call | tf_op jit(solution)/shard_map/last_out/pallas_call | solution.py:232
  (127 shorter events, 21.0 us)
Async XLA Ops:
  0.6 12.3 %copy-start.1 = (bf16[768,768]{1,0:T(8,128)(2,1)S(1)}, bf16[768,768]{1,0:T(8,128)(2,1)}, u32[]{:S(2)}) copy-start(bf16[768,768]{1,0:T(8,128)(2,1)} %refs_0_.1) | copy-start | bytes 3538948
  0.7 12.3 %copy-start.2 = (bf16[768,768]{1,0:T(8,128)(2,1)S(1)}, bf16[768,768]{1,0:T(8,128)(2,1)}, u32[]{:S(2)}) copy-start(bf16[768,768]{1,0:T(8,128)(2,1)} %refs_1_.3) | copy-start | bytes 3538948
  0.7 12.3 %copy-start.14 = (bf16[4,1,384,768]{3,2,1,0:T(8,128)(2,1)S(1)}, bf16[4,1,384,768]{3,2,1,0:T(8,128)(2,1)}, u32[]{:S(2)}) copy-start(bf16[4,1,384,768]{3,2,1,0:T(8,128)(2,1)} %param.18) | copy-start | bytes 7077892
  7.0 23.0 %collective-permute-start.4 = (bf16[128,768]{1,0:T(8,128)(2,1)}, bf16[128,768]{1,0:T(8,128)(2,1)S(1)}, u32[]{:S(2)}, u32[]{:S(2)}) collective-permute-start(bf16[128,768]{1,0:T(8,128)(2,1)} %get-tuple-element.127.refs_3_), channel_id=1, source_target_pairs={{0,3},{1,2},{2,1},{3,0},{4,7},{5,6},{6,5},{7,4},{8,11},{9,10},{10,... | collective-permute-start | bytes 589832 | tf_op jit(solution)/shard_map/ppermute | solution.py:944
  8.3 19.5 %collective-permute-start.2 = (bf16[128,768]{1,0:T(8,128)(2,1)}, bf16[128,768]{1,0:T(8,128)(2,1)S(1)}, u32[]{:S(2)}, u32[]{:S(2)}) collective-permute-start(bf16[128,768]{1,0:T(8,128)(2,1)} %get-tuple-element.127.refs_3_), channel_id=1, source_target_pairs={{0,2},{1,3},{2,0},{3,1},{4,6},{5,7},{6,4},{7,5},{8,10},{9,11},{10,... | collective-permute-start | bytes 589832 | tf_op jit(solution)/shard_map/ppermute | solution.py:944
  9.4 14.2 %collective-permute-start = (bf16[128,768]{1,0:T(8,128)(2,1)}, bf16[128,768]{1,0:T(8,128)(2,1)S(1)}, u32[]{:S(2)}, u32[]{:S(2)}) collective-permute-start(bf16[128,768]{1,0:T(8,128)(2,1)} %get-tuple-element.127.refs_3_), channel_id=1, source_target_pairs={{0,1},{1,0},{2,3},{3,2},{4,5},{5,4},{6,7},{7,6},{8,9},{9,8},{10,11... | collective-permute-start | bytes 589832 | tf_op jit(solution)/shard_map/ppermute | solution.py:944
  10.5 19.8 %collective-permute-start.5 = (bf16[128,1536]{1,0:T(8,128)(2,1)}, bf16[128,1536]{1,0:T(8,128)(2,1)S(1)}, u32[]{:S(2)}, u32[]{:S(2)}) collective-permute-start(bf16[128,1536]{1,0:T(8,128)(2,1)} %get-tuple-element.135), channel_id=1, source_target_pairs={{0,8},{4,12},{8,0},{12,4},{16,24},{20,28},{24,16},{28,20},{1,9},{5... | collective-permute-start | bytes 1179656 | tf_op jit(solution)/shard_map/ppermute | solution.py:944
  11.7 18.6 %collective-permute-start.6 = (bf16[128,1536]{1,0:T(8,128)(2,1)}, bf16[128,1536]{1,0:T(8,128)(2,1)S(1)}, u32[]{:S(2)}, u32[]{:S(2)}) collective-permute-start(bf16[128,1536]{1,0:T(8,128)(2,1)} %get-tuple-element.136), channel_id=1, source_target_pairs={{0,16},{4,20},{8,24},{12,28},{16,0},{20,4},{24,8},{28,12},{1,17},{... | collective-permute-start | bytes 1179656 | tf_op jit(solution)/shard_map/ppermute | solution.py:944
  23.6 11.1 %collective-permute-start.8 = (bf16[128,1536]{1,0:T(8,128)(2,1)S(1)}, bf16[128,1536]{1,0:T(8,128)(2,1)S(1)}, u32[]{:S(2)}, u32[]{:S(2)}) collective-permute-start(bf16[128,1536]{1,0:T(8,128)(2,1)S(1)} %copy-done.25), channel_id=1, source_target_pairs={{0,24},{4,28},{8,16},{12,20},{16,8},{20,12},{24,0},{28,4},{1,25},{... | collective-permute-start | bytes 1179656 | tf_op jit(solution)/shard_map/ppermute | solution.py:944
  27.8 22.2 %slice-start = ((s8[4718592]{0:T(1024)(128)(4,1)}), s8[4194304]{0:T(1024)(128)(4,1)S(1)}, s32[]{:S(2)}) async-start(s8[4718592]{0:T(1024)(128)(4,1)} %bitcast.24), calls=%async_computation | async-start | bytes 8388608
  27.8 22.2 %slice-start.2 = ((s8[4718592]{0:T(1024)(128)(4,1)}), s8[4194304]{0:T(1024)(128)(4,1)S(1)}, s32[]{:S(2)}) async-start(s8[4718592]{0:T(1024)(128)(4,1)} %bitcast.26), calls=%async_computation.2 | async-start | bytes 8388608
  29.9 11.7 %collective-permute-start.3 = (bf16[128,896]{1,0:T(8,128)(2,1)S(1)}, bf16[128,896]{1,0:T(8,128)(2,1)S(1)}, u32[]{:S(2)}, u32[]{:S(2)}) collective-permute-start(bf16[128,896]{1,0:T(8,128)(2,1)S(1)} %get-tuple-element.133), channel_id=1, source_target_pairs={{0,2},{1,3},{2,0},{3,1},{4,6},{5,7},{6,4},{7,5},{8,10},{9,11},{10,... | collective-permute-start | bytes 688136 | tf_op jit(solution)/shard_map/ppermute | solution.py:944
  30.0 11.6 %collective-permute-start.1 = (bf16[128,896]{1,0:T(8,128)(2,1)S(1)}, bf16[128,896]{1,0:T(8,128)(2,1)S(1)}, u32[]{:S(2)}, u32[]{:S(2)}) collective-permute-start(bf16[128,896]{1,0:T(8,128)(2,1)S(1)} %get-tuple-element.131), channel_id=1, source_target_pairs={{0,1},{1,0},{2,3},{3,2},{4,5},{5,4},{6,7},{7,6},{8,9},{9,8},{10,11... | collective-permute-start | bytes 688136 | tf_op jit(solution)/shard_map/ppermute | solution.py:944
  30.3 19.7 %slice-start.1 = ((s8[4718592]{0:T(1024)(128)(4,1)}), s8[524288]{0:T(1024)(128)(4,1)S(1)}, s32[]{:S(2)}) async-start(s8[4718592]{0:T(1024)(128)(4,1)} %bitcast.24), calls=%async_computation.1 | async-start | bytes 1048576
  30.3 19.7 %slice-start.3 = ((s8[4718592]{0:T(1024)(128)(4,1)}), s8[524288]{0:T(1024)(128)(4,1)S(1)}, s32[]{:S(2)}) async-start(s8[4718592]{0:T(1024)(128)(4,1)} %bitcast.26), calls=%async_computation.3 | async-start | bytes 1048576
  32.4 17.6 %collective-permute-start.7 = (bf16[128,896]{1,0:T(8,128)(2,1)S(1)}, bf16[128,896]{1,0:T(8,128)(2,1)S(1)}, u32[]{:S(2)}, u32[]{:S(2)}) collective-permute-start(bf16[128,896]{1,0:T(8,128)(2,1)S(1)} %get-tuple-element.137), channel_id=1, source_target_pairs={{0,3},{1,2},{2,1},{3,0},{4,7},{5,6},{6,5},{7,4},{8,11},{9,10},{10,... | collective-permute-start | bytes 688136 | tf_op jit(solution)/shard_map/ppermute | solution.py:944
  41.6 8.4 %copy-start.17 = (f32[128,768]{1,0:T(8,128)S(1)}, f32[128,768]{1,0:T(8,128)}, u32[]{:S(2)}) copy-start(f32[128,768]{1,0:T(8,128)} %get-tuple-element.122.refs_0_.refs_1_) | copy-start | bytes 1179652
  58.9 9.0 %collective-permute-start.9 = (bf16[128,896]{1,0:T(8,128)(2,1)S(1)}, bf16[128,896]{1,0:T(8,128)(2,1)S(1)}, u32[]{:S(2)}, u32[]{:S(2)}) collective-permute-start(bf16[128,896]{1,0:T(8,128)(2,1)S(1)} %get-tuple-element.149.refs_4_), channel_id=1, source_target_pairs={{0,1},{1,0},{2,3},{3,2},{4,5},{5,4},{6,7},{7,6},{8,9},{9,8},{10,11... | collective-permute-start | bytes 688136 | tf_op jit(solution)/shard_map/ppermute | solution.py:944
  58.9 17.8 %collective-permute-start.11 = (bf16[128,896]{1,0:T(8,128)(2,1)S(1)}, bf16[128,896]{1,0:T(8,128)(2,1)S(1)}, u32[]{:S(2)}, u32[]{:S(2)}) collective-permute-start(bf16[128,896]{1,0:T(8,128)(2,1)S(1)} %get-tuple-element.149.refs_4_), channel_id=1, source_target_pairs={{0,2},{1,3},{2,0},{3,1},{4,6},{5,7},{6,4},{7,5},{8,10},{9,11},{10,... | collective-permute-start | bytes 688136 | tf_op jit(solution)/shard_map/ppermute | solution.py:944
  62.3 19.3 %collective-permute-start.13 = (bf16[128,896]{1,0:T(8,128)(2,1)S(1)}, bf16[128,896]{1,0:T(8,128)(2,1)S(1)}, u32[]{:S(2)}, u32[]{:S(2)}) collective-permute-start(bf16[128,896]{1,0:T(8,128)(2,1)S(1)} %get-tuple-element.149.refs_4_), channel_id=1, source_target_pairs={{0,3},{1,2},{2,1},{3,0},{4,7},{5,6},{6,5},{7,4},{8,11},{9,10},{10,... | collective-permute-start | bytes 688136 | tf_op jit(solution)/shard_map/ppermute | solution.py:944
  62.3 34.8 %collective-permute-start.15 = (bf16[128,3072]{1,0:T(8,128)(2,1)S(1)}, bf16[128,3072]{1,0:T(8,128)(2,1)S(1)}, u32[]{:S(2)}, u32[]{:S(2)}) collective-permute-start(bf16[128,3072]{1,0:T(8,128)(2,1)S(1)} %get-tuple-element.162), channel_id=1, source_target_pairs={{0,8},{4,12},{8,0},{12,4},{16,24},{20,28},{24,16},{28,20},{1,9},{5... | collective-permute-start | bytes 2359304 | tf_op jit(solution)/shard_map/ppermute | solution.py:944
  62.8 35.5 %collective-permute-start.16 = (bf16[128,3072]{1,0:T(8,128)(2,1)S(1)}, bf16[128,3072]{1,0:T(8,128)(2,1)S(1)}, u32[]{:S(2)}, u32[]{:S(2)}) collective-permute-start(bf16[128,3072]{1,0:T(8,128)(2,1)S(1)} %get-tuple-element.163), channel_id=1, source_target_pairs={{0,16},{4,20},{8,24},{12,28},{16,0},{20,4},{24,8},{28,12},{1,17},{... | collective-permute-start | bytes 2359304 | tf_op jit(solution)/shard_map/ppermute | solution.py:944
  67.9 32.5 %collective-permute-start.17 = (bf16[128,3072]{1,0:T(8,128)(2,1)S(1)}, bf16[128,3072]{1,0:T(8,128)(2,1)S(1)}, u32[]{:S(2)}, u32[]{:S(2)}) collective-permute-start(bf16[128,3072]{1,0:T(8,128)(2,1)S(1)} %get-tuple-element.164), channel_id=1, source_target_pairs={{0,24},{4,28},{8,16},{12,20},{16,8},{20,12},{24,0},{28,4},{1,25},{... | collective-permute-start | bytes 2359304 | tf_op jit(solution)/shard_map/ppermute | solution.py:944
  84.3 17.9 %collective-permute-start.14 = (bf16[128,768]{1,0:T(8,128)(2,1)S(1)}, bf16[128,768]{1,0:T(8,128)(2,1)S(1)}, u32[]{:S(2)}, u32[]{:S(2)}) collective-permute-start(bf16[128,768]{1,0:T(8,128)(2,1)S(1)} %get-tuple-element.159), channel_id=1, source_target_pairs={{0,3},{1,2},{2,1},{3,0},{4,7},{5,6},{6,5},{7,4},{8,11},{9,10},{10,... | collective-permute-start | bytes 589832 | tf_op jit(solution)/shard_map/ppermute | solution.py:944
  86.6 17.0 %collective-permute-start.12 = (bf16[128,768]{1,0:T(8,128)(2,1)S(1)}, bf16[128,768]{1,0:T(8,128)(2,1)S(1)}, u32[]{:S(2)}, u32[]{:S(2)}) collective-permute-start(bf16[128,768]{1,0:T(8,128)(2,1)S(1)} %get-tuple-element.157), channel_id=1, source_target_pairs={{0,2},{1,3},{2,0},{3,1},{4,6},{5,7},{6,4},{7,5},{8,10},{9,11},{10,... | collective-permute-start | bytes 589832 | tf_op jit(solution)/shard_map/ppermute | solution.py:944
  90.7 9.8 %copy-start = (bf16[128,1536]{1,0:T(8,128)(2,1)S(1)}, bf16[128,1536]{1,0:T(8,128)(2,1)}, u32[]{:S(2)}) copy-start(bf16[128,1536]{1,0:T(8,128)(2,1)} %get-tuple-element.160.refs_0_) | copy-start | bytes 1179652
  97.1 10.0 %collective-permute-start.10 = (bf16[128,768]{1,0:T(8,128)(2,1)S(1)}, bf16[128,768]{1,0:T(8,128)(2,1)S(1)}, u32[]{:S(2)}, u32[]{:S(2)}) collective-permute-start(bf16[128,768]{1,0:T(8,128)(2,1)S(1)} %get-tuple-element.155), channel_id=1, source_target_pairs={{0,1},{1,0},{2,3},{3,2},{4,5},{5,4},{6,7},{7,6},{8,9},{9,8},{10,11... | collective-permute-start | bytes 589832 | tf_op jit(solution)/shard_map/ppermute | solution.py:944
  98.4 5.3 %collective-permute-start.19 = (bf16[4,96,1536]{2,1,0:T(8,128)(2,1)S(1)}, bf16[4,96,1536]{2,1,0:T(8,128)(2,1)S(1)}, u32[]{:S(2)}, u32[]{:S(2)}) collective-permute-start(bf16[4,96,1536]{2,1,0:T(8,128)(2,1)S(1)} %get-tuple-element.179), channel_id=1, source_target_pairs={{0,4},{4,0},{8,12},{12,8},{16,20},{20,16},{24,28},{28,24},{1,5},{5... | collective-permute-start | bytes 3538952 | tf_op jit(solution)/shard_map/ppermute | solution.py:944
  102.1 3.8 %collective-permute-start.18 = (bf16[4,96,1536]{2,1,0:T(8,128)(2,1)S(1)}, bf16[4,96,1536]{2,1,0:T(8,128)(2,1)S(1)}, u32[]{:S(2)}, u32[]{:S(2)}) collective-permute-start(bf16[4,96,1536]{2,1,0:T(8,128)(2,1)S(1)} %get-tuple-element.177), channel_id=1, source_target_pairs={{0,4},{4,0},{8,12},{12,8},{16,20},{20,16},{24,28},{28,24},{1,5},{5... | collective-permute-start | bytes 3538952 | tf_op jit(solution)/shard_map/ppermute | solution.py:944
  104.4 14.5 %collective-permute-start.24 = (bf16[2,4,96,384]{3,2,1,0:T(8,128)(2,1)S(1)}, bf16[2,4,96,384]{3,2,1,0:T(8,128)(2,1)S(1)}, u32[]{:S(2)}, u32[]{:S(2)}) collective-permute-start(bf16[2,4,96,384]{3,2,1,0:T(8,128)(2,1)S(1)} %get-tuple-element.192), channel_id=1, source_target_pairs={{0,8},{4,12},{8,0},{12,4},{16,24},{20,28},{24,16},{28,20},{1,9},{5... | collective-permute-start | bytes 1769480 | tf_op jit(solution)/shard_map/ppermute | solution.py:944
  106.3 14.5 %collective-permute-start.23 = (bf16[2,96,1536]{2,1,0:T(8,128)(2,1)S(1)}, bf16[2,96,1536]{2,1,0:T(8,128)(2,1)S(1)}, u32[]{:S(2)}, u32[]{:S(2)}) collective-permute-start(bf16[2,96,1536]{2,1,0:T(8,128)(2,1)S(1)} %get-tuple-element.190), channel_id=1, source_target_pairs={{0,1},{1,0},{2,3},{3,2},{4,5},{5,4},{6,7},{7,6},{8,9},{9,8},{10,11... | collective-permute-start | bytes 1769480 | tf_op jit(solution)/shard_map/ppermute | solution.py:944
  113.2 12.4 %collective-permute-start.20 = (bf16[136,1152]{1,0:T(8,128)(2,1)S(1)}, bf16[136,1152]{1,0:T(8,128)(2,1)S(1)}, u32[]{:S(2)}, u32[]{:S(2)}) collective-permute-start(bf16[136,1152]{1,0:T(8,128)(2,1)S(1)} %get-tuple-element.186), channel_id=1, source_target_pairs={{0,8},{4,12},{8,0},{12,4},{16,24},{20,28},{24,16},{28,20},{1,9},{5... | collective-permute-start | bytes 940040 | tf_op jit(solution)/shard_map/ppermute | solution.py:944
  114.5 11.1 %collective-permute-start.21 = (bf16[136,1152]{1,0:T(8,128)(2,1)S(1)}, bf16[136,1152]{1,0:T(8,128)(2,1)S(1)}, u32[]{:S(2)}, u32[]{:S(2)}) collective-permute-start(bf16[136,1152]{1,0:T(8,128)(2,1)S(1)} %get-tuple-element.187), channel_id=1, source_target_pairs={{0,16},{4,20},{8,24},{12,28},{16,0},{20,4},{24,8},{28,12},{1,17},{... | collective-permute-start | bytes 940040 | tf_op jit(solution)/shard_map/ppermute | solution.py:944
  115.2 18.5 %collective-permute-start.22 = (bf16[136,1152]{1,0:T(8,128)(2,1)S(1)}, bf16[136,1152]{1,0:T(8,128)(2,1)S(1)}, u32[]{:S(2)}, u32[]{:S(2)}) collective-permute-start(bf16[136,1152]{1,0:T(8,128)(2,1)S(1)} %get-tuple-element.188), channel_id=1, source_target_pairs={{0,24},{4,28},{8,16},{12,20},{16,8},{20,12},{24,0},{28,4},{1,25},{... | collective-permute-start | bytes 940040 | tf_op jit(solution)/shard_map/ppermute | solution.py:944
  119.1 17.6 %collective-permute-start.26 = (bf16[1,4,96,384]{3,2,1,0:T(8,128)(2,1)S(1)}, bf16[1,4,96,384]{3,2,1,0:T(8,128)(2,1)S(1)}, u32[]{:S(2)}, u32[]{:S(2)}) collective-permute-start(bf16[1,4,96,384]{3,2,1,0:T(8,128)(2,1)S(1)} %get-tuple-element.199), channel_id=1, source_target_pairs={{0,16},{4,20},{8,24},{12,28},{16,0},{20,4},{24,8},{28,12},{1,17},{... | collective-permute-start | bytes 884744 | tf_op jit(solution)/shard_map/ppermute | solution.py:944
  120.9 15.8 %collective-permute-start.27 = (bf16[1,96,1536]{2,1,0:T(8,128)(2,1)S(1)}, bf16[1,96,1536]{2,1,0:T(8,128)(2,1)S(1)}, u32[]{:S(2)}, u32[]{:S(2)}) collective-permute-start(bf16[1,96,1536]{2,1,0:T(8,128)(2,1)S(1)} %get-tuple-element.201), channel_id=1, source_target_pairs={{0,2},{1,3},{2,0},{3,1},{4,6},{5,7},{6,4},{7,5},{8,10},{9,11},{10,... | collective-permute-start | bytes 884744 | tf_op jit(solution)/shard_map/ppermute | solution.py:944
  135.3 3.5 %collective-permute-start.25 = (bf16[4,104,1152]{2,1,0:T(8,128)(2,1)S(1)}, bf16[4,104,1152]{2,1,0:T(8,128)(2,1)S(1)}, u32[]{:S(2)}, u32[]{:S(2)}) collective-permute-start(bf16[4,104,1152]{2,1,0:T(8,128)(2,1)S(1)} %get-tuple-element.197), channel_id=1, source_target_pairs={{0,4},{4,0},{8,12},{12,8},{16,20},{20,16},{24,28},{28,24},{1,5},{5... | collective-permute-start | bytes 2875400 | tf_op jit(solution)/shard_map/ppermute | solution.py:944
  139.1 14.5 %collective-permute-start.28 = (bf16[104,1536]{1,0:T(8,128)(2,1)S(1)}, bf16[104,1536]{1,0:T(8,128)(2,1)S(1)}, u32[]{:S(2)}, u32[]{:S(2)}) collective-permute-start(bf16[104,1536]{1,0:T(8,128)(2,1)S(1)} %get-tuple-element.203), channel_id=1, source_target_pairs={{0,1},{1,0},{2,3},{3,2},{4,5},{5,4},{6,7},{7,6},{8,9},{9,8},{10,11... | collective-permute-start | bytes 958472 | tf_op jit(solution)/shard_map/ppermute | solution.py:944
  140.6 21.3 %collective-permute-start.29 = (bf16[104,1536]{1,0:T(8,128)(2,1)S(1)}, bf16[104,1536]{1,0:T(8,128)(2,1)S(1)}, u32[]{:S(2)}, u32[]{:S(2)}) collective-permute-start(bf16[104,1536]{1,0:T(8,128)(2,1)S(1)} %get-tuple-element.204), channel_id=1, source_target_pairs={{0,2},{1,3},{2,0},{3,1},{4,6},{5,7},{6,4},{7,5},{8,10},{9,11},{10,... | collective-permute-start | bytes 958472 | tf_op jit(solution)/shard_map/ppermute | solution.py:944
  142.0 27.6 %collective-permute-start.30 = (bf16[104,1536]{1,0:T(8,128)(2,1)S(1)}, bf16[104,1536]{1,0:T(8,128)(2,1)S(1)}, u32[]{:S(2)}, u32[]{:S(2)}) collective-permute-start(bf16[104,1536]{1,0:T(8,128)(2,1)S(1)} %get-tuple-element.205), channel_id=1, source_target_pairs={{0,3},{1,2},{2,1},{3,0},{4,7},{5,6},{6,5},{7,4},{8,11},{9,10},{10,... | collective-permute-start | bytes 958472 | tf_op jit(solution)/shard_map/ppermute | solution.py:944
  142.1 30.7 %collective-permute-start.36 = (bf16[96,1536]{1,0:T(8,128)(2,1)S(1)}, bf16[96,1536]{1,0:T(8,128)(2,1)S(1)}, u32[]{:S(2)}, u32[]{:S(2)}) collective-permute-start(bf16[96,1536]{1,0:T(8,128)(2,1)S(1)} %get-tuple-element.210.refs_0_), channel_id=1, source_target_pairs={{0,24},{4,28},{8,16},{12,20},{16,8},{20,12},{24,0},{28,4},{1,25},{... | collective-permute-start | bytes 884744 | tf_op jit(solution)/shard_map/ppermute | solution.py:944
  143.4 29.4 %collective-permute-start.35 = (bf16[96,1536]{1,0:T(8,128)(2,1)S(1)}, bf16[96,1536]{1,0:T(8,128)(2,1)S(1)}, u32[]{:S(2)}, u32[]{:S(2)}) collective-permute-start(bf16[96,1536]{1,0:T(8,128)(2,1)S(1)} %get-tuple-element.210.refs_0_), channel_id=1, source_target_pairs={{0,16},{4,20},{8,24},{12,28},{16,0},{20,4},{24,8},{28,12},{1,17},{... | collective-permute-start | bytes 884744 | tf_op jit(solution)/shard_map/ppermute | solution.py:944
  153.6 19.1 %collective-permute-start.34 = (bf16[96,1536]{1,0:T(8,128)(2,1)S(1)}, bf16[96,1536]{1,0:T(8,128)(2,1)S(1)}, u32[]{:S(2)}, u32[]{:S(2)}) collective-permute-start(bf16[96,1536]{1,0:T(8,128)(2,1)S(1)} %get-tuple-element.210.refs_0_), channel_id=1, source_target_pairs={{0,8},{4,12},{8,0},{12,4},{16,24},{20,28},{24,16},{28,20},{1,9},{5... | collective-permute-start | bytes 884744 | tf_op jit(solution)/shard_map/ppermute | solution.py:944
  169.9 8.1 %collective-permute-start.33 = (bf16[96,1536]{1,0:T(8,128)(2,1)S(1)}, bf16[96,1536]{1,0:T(8,128)(2,1)S(1)}, u32[]{:S(2)}, u32[]{:S(2)}) collective-permute-start(bf16[96,1536]{1,0:T(8,128)(2,1)S(1)} %get-tuple-element.209.refs_0_), channel_id=1, source_target_pairs={{0,24},{4,28},{8,16},{12,20},{16,8},{20,12},{24,0},{28,4},{1,25},{... | collective-permute-start | bytes 884744 | tf_op jit(solution)/shard_map/ppermute | solution.py:944
  170.9 15.1 %collective-permute-start.32 = (bf16[96,1536]{1,0:T(8,128)(2,1)S(1)}, bf16[96,1536]{1,0:T(8,128)(2,1)S(1)}, u32[]{:S(2)}, u32[]{:S(2)}) collective-permute-start(bf16[96,1536]{1,0:T(8,128)(2,1)S(1)} %get-tuple-element.209.refs_0_), channel_id=1, source_target_pairs={{0,16},{4,20},{8,24},{12,28},{16,0},{20,4},{24,8},{28,12},{1,17},{... | collective-permute-start | bytes 884744 | tf_op jit(solution)/shard_map/ppermute | solution.py:944
  172.8 13.3 %collective-permute-start.31 = (bf16[96,1536]{1,0:T(8,128)(2,1)S(1)}, bf16[96,1536]{1,0:T(8,128)(2,1)S(1)}, u32[]{:S(2)}, u32[]{:S(2)}) collective-permute-start(bf16[96,1536]{1,0:T(8,128)(2,1)S(1)} %get-tuple-element.209.refs_0_), channel_id=1, source_target_pairs={{0,8},{4,12},{8,0},{12,4},{16,24},{20,28},{24,16},{28,20},{1,9},{5... | collective-permute-start | bytes 884744 | tf_op jit(solution)/shard_map/ppermute | solution.py:944
  172.9 14.4 %collective-permute-start.38 = (bf16[4,96,1536]{2,1,0:T(8,128)(2,1)S(1)}, bf16[4,96,1536]{2,1,0:T(8,128)(2,1)S(1)}, u32[]{:S(2)}, u32[]{:S(2)}) collective-permute-start(bf16[4,96,1536]{2,1,0:T(8,128)(2,1)S(1)} %get-tuple-element.214.refs_0_), channel_id=1, source_target_pairs={{0,4},{4,0},{8,12},{12,8},{16,20},{20,16},{24,28},{28,24},{1,5},{5... | collective-permute-start | bytes 3538952 | tf_op jit(solution)/shard_map/ppermute | solution.py:944
  186.2 3.8 %collective-permute-start.37 = (bf16[4,96,1536]{2,1,0:T(8,128)(2,1)S(1)}, bf16[4,96,1536]{2,1,0:T(8,128)(2,1)S(1)}, u32[]{:S(2)}, u32[]{:S(2)}) collective-permute-start(bf16[4,96,1536]{2,1,0:T(8,128)(2,1)S(1)} %get-tuple-element.213.refs_0_), channel_id=1, source_target_pairs={{0,4},{4,0},{8,12},{12,8},{16,20},{20,16},{24,28},{28,24},{1,5},{5... | collective-permute-start | bytes 3538952 | tf_op jit(solution)/shard_map/ppermute | solution.py:944
  (21 other events, 86.2 us)
